TPU v7x, 256 devices: a whole 4x4x8 slice. The times are simulated.
256 devices in a mesh: ulysses: 8 (over x, core), blk: 32 (over y, z).
Axes of the slice: x: 4, y: 4, z: 8, core: 2. Of those that a mesh axis runs over, the one named last changes fastest.
Arguments:
- query: bfloat16 [49152, 8, 128], P(('blk', 'ulysses')), may hold values from -6 to 6
- key: bfloat16 [49152, 128], P(('blk', 'ulysses')), may hold values from -6 to 6
- value: bfloat16 [49152, 128], P(('blk', 'ulysses')), may hold values from -6 to 6
- output: bfloat16 [49152, 8, 128], P(('blk', 'ulysses')), may hold values from -0.59765625 to 0.59765625
- grad_out: bfloat16 [49152, 8, 128], P(('blk', 'ulysses')), may hold values from -6 to 6
- lse: float32 [8, 49152], P(None, ('blk', 'ulysses')), may hold values from 4 to 7
- doc_lengths: int32 [32], replicated, may hold values from 1 to 3072, 49152 in all
Outputs:
- grad_query: bfloat16 [49152, 8, 128], P(('blk', 'ulysses'))
- grad_key: bfloat16 [49152, 128], P(('blk', 'ulysses'))
- grad_value: bfloat16 [49152, 128], P(('blk', 'ulysses'))
Inputs may be any that keep to these rules, and one draw needn't show every extreme that they name: `doc_lengths`: the documents are laid end to end from position 0 and fill all 49152 positions; the longest has exactly 3072 tokens.
All inputs are finite; a program needn't handle non-finite values.
Results may differ from a plain program's by a relative error of at most 0.024.
Values may be sent and summed in bfloat16 or wider, within the bound.
A program may use at most 64 MiB of HBM per device.

v0:
```python
import math

import jax
import jax.numpy as jnp
from jax import lax
from jax.sharding import PartitionSpec as P

REACH = 2


def shifted(block, axis, distance):
    devices = range(lax.axis_size(axis))
    route = [(i - distance, i) for i in devices if i - distance in devices]
    return lax.ppermute(block, axis, route)


def from_behind(value, axis, steps):
    count = lax.axis_size(axis)
    pairs = [(source, (source + steps) % count) for source in range(count)]
    return lax.ppermute(value, axis, pairs)


def doc_ids(positions, ends):
    return jnp.sum((ends[None, :] <= positions[:, None]).astype(jnp.int32), axis=1)


def block_grads(queries, douts, stats, kv_now, qpos, kpos, ends, qblock, scale):
    block = queries.shape[0]
    heads = queries.shape[1]
    width = queries.shape[2]
    nblocks = block // qblock
    key_rows = kv_now[0]
    val_rows = kv_now[1]
    key_doc = doc_ids(kpos, ends)
    query_doc = doc_ids(qpos, ends)
    inputs = (
        queries.reshape(nblocks, qblock, heads, width),
        douts.reshape(nblocks, qblock, heads, width),
        stats[0].reshape(nblocks, qblock, heads),
        stats[1].reshape(nblocks, qblock, heads),
        qpos.reshape(nblocks, qblock),
        query_doc.reshape(nblocks, qblock),
    )

    def one(carry, pieces):
        qpart, dpart, lpart, epart, qp, qdoc = pieces
        allowed = (
            (qdoc[:, None] == key_doc[None, :])
            & (kpos[None, :] <= qp[:, None])
            & (kpos[None, :] >= 0)
        )
        scores = (
            jnp.einsum("qhd,kd->hqk", qpart, key_rows, preferred_element_type=jnp.float32) * scale
        )
        probs = jnp.where(allowed[None], jnp.exp(scores - lpart.T[:, :, None]), 0.0)
        rounded = probs.astype(jnp.bfloat16)
        dv_term = jnp.einsum("hqk,qhd->kd", rounded, dpart, preferred_element_type=jnp.float32)
        dprobs = jnp.einsum("qhd,kd->hqk", dpart, val_rows, preferred_element_type=jnp.float32)
        dscores = (probs * (dprobs - epart.T[:, :, None])).astype(jnp.bfloat16)
        dq_part = jnp.einsum("hqk,kd->qhd", dscores, key_rows, preferred_element_type=jnp.float32)
        dk_term = jnp.einsum("hqk,qhd->kd", dscores, qpart, preferred_element_type=jnp.float32)
        return (carry + jnp.stack([dk_term, dv_term]), dq_part)

    total, dq_blocks = lax.scan(one, jnp.zeros((2, block, width), jnp.float32), inputs)
    return (dq_blocks.reshape(block, heads, width), total)


def per_device(query, key, value, output, grad_out, lse, doc_lengths):
    groups = lax.axis_size("ulysses")
    tokens = query.shape[0]
    block = tokens * groups
    scale = query.shape[2] ** (-0.5)
    delta = jnp.einsum("thd,thd->th", grad_out, output, preferred_element_type=jnp.float32)
    stats = lax.all_to_all(
        jnp.stack([lse.T, delta]), "ulysses", split_axis=2, concat_axis=1, tiled=True
    )
    queries, douts = (
        lax.all_to_all(query, "ulysses", split_axis=1, concat_axis=0, tiled=True),
        lax.all_to_all(grad_out, "ulysses", split_axis=1, concat_axis=0, tiled=True),
    )
    kv_own = jnp.stack([key, value])
    kv_local = lax.all_gather(kv_own, "ulysses", axis=1, tiled=True)
    ends = jnp.cumsum(doc_lengths)
    offsets = jnp.arange(block, dtype=jnp.int32)
    base = lax.axis_index("blk") * block
    qpos = base + offsets
    qblock = math.gcd(block, 512)

    def grads_at(kv_now, back):
        kpos = base - back * block + offsets
        return block_grads(queries, douts, stats, kv_now, qpos, kpos, ends, qblock, scale)

    dq_sum, term = grads_at(kv_local, 0)
    total = term
    kv_now = kv_local
    for back in range(1, REACH + 1):
        kv_now = shifted(kv_now, "blk", 1)
        total = from_behind(total, "blk", 1)
        dq_part, term = grads_at(kv_now, back)
        dq_sum = dq_sum + dq_part
        total = total + term
    total = from_behind(total, "blk", -REACH)
    total = lax.psum_scatter(total, "ulysses", scatter_dimension=1, tiled=True)
    grad_key = (total[0] * scale).astype(jnp.bfloat16)
    grad_value = total[1].astype(jnp.bfloat16)
    grad_query = lax.all_to_all(
        (dq_sum * scale).astype(jnp.bfloat16), "ulysses", split_axis=0, concat_axis=1, tiled=True
    )
    return (grad_query, grad_key, grad_value)


def solution(mesh):
    return jax.shard_map(
        per_device,
        mesh=mesh,
        in_specs=(
            P(("blk", "ulysses"), None, None),
            P(("blk", "ulysses"), None),
            P(("blk", "ulysses"), None),
            P(("blk", "ulysses"), None, None),
            P(("blk", "ulysses"), None, None),
            P(None, ("blk", "ulysses")),
            P(),
        ),
        out_specs=(
            P(("blk", "ulysses"), None, None),
            P(("blk", "ulysses"), None),
            P(("blk", "ulysses"), None),
        ),
        check_vma=False,
    )
```

profile of v0, /device:TPU:24, one launch (start us, length us, event | category | flops | bytes accessed | tf_op | source)
XLA Modules:
  0.0 306.1 jit_solution(8753124329271880849)
XLA Ops:
  8.1 14.8 %all_gather.3 = bf16[2,1536,128]{2,1,0:T(8,128)(2,1)} all-gather(bf16[2,192,128]{2,1,0:T(8,128)(2,1)S(1)} %pad_maximum_fusion), channel_id=1, replica_groups=mesh['ulysses'=8,'blk'=32] {'ulysses'}, dimensions={1}, use_global_device_ids=true | all-gather | bytes 884736 | tf_op jit(solution)/shard_map/all_gather | solution.py:82
  22.9 3.8 %collective-permute-start = (bf16[2,1536,128]{2,1,0:T(8,128)(2,1)}, bf16[2,1536,128]{2,1,0:T(8,128)(2,1)}, u32[]{:S(2)}, u32[]{:S(2)}) collective-permute-start(bf16[2,1536,128]{2,1,0:T(8,128)(2,1)} %all_gather.3), channel_id=1, source_target_pairs={{0,1},{1,2},{2,3},{3,4},{4,5},{5,6},{6,7},{7,8},{8,9},{9,10},{10,1... | collective-permute-start | bytes 2359304 | tf_op jit(solution)/shard_map/ppermute | solution.py:14
  28.9 3.7 %all-to-all-start.1 = ((f32[2,192,8]{1,0,2:T(2,128)}), f32[2,192,8]{1,0,2:T(2,128)S(1)}, u32[]{:S(2)}, u32[]{:S(2)}) async-start(f32[2,192,8]{1,0,2:T(2,128)} %pad_maximum_fusion.1), calls=%async_computation.1 | async-start | bytes 32768 | tf_op jit(solution)/shard_map/all_to_all | solution.py:74
  34.5 3.4 %all-to-all-done.1 = f32[2,192,8]{1,0,2:T(2,128)S(1)} async-done(((f32[2,192,8]{1,0,2:T(2,128)}), f32[2,192,8]{1,0,2:T(2,128)S(1)}, u32[]{:S(2)}, u32[]{:S(2)}) %all-to-all-start.1) | async-done | bytes 12320 | tf_op jit(solution)/shard_map/all_to_all | solution.py:74
  37.9 3.5 %all-to-all-start.2 = ((bf16[192,8,128]{2,0,1:T(8,128)(2,1)}), bf16[192,8,128]{2,0,1:T(8,128)(2,1)S(1)}, u32[]{:S(2)}, u32[]{:S(2)}) async-start(bf16[192,8,128]{2,0,1:T(8,128)(2,1)} %copy.61), calls=%async_computation.2 | async-start | bytes 786432 | tf_op jit(solution)/shard_map/all_to_all | solution.py:79
  43.4 6.9 %all-to-all-done.2 = bf16[192,8,128]{2,0,1:T(8,128)(2,1)S(1)} async-done(((bf16[192,8,128]{2,0,1:T(8,128)(2,1)}), bf16[192,8,128]{2,0,1:T(8,128)(2,1)S(1)}, u32[]{:S(2)}, u32[]{:S(2)}) %all-to-all-start.2) | async-done | bytes 393248 | tf_op jit(solution)/shard_map/all_to_all | solution.py:79
  50.3 3.5 %all-to-all-start = ((bf16[192,8,128]{2,0,1:T(8,128)(2,1)}), bf16[192,8,128]{2,0,1:T(8,128)(2,1)S(1)}, u32[]{:S(2)}, u32[]{:S(2)}) async-start(bf16[192,8,128]{2,0,1:T(8,128)(2,1)} %copy.60), calls=%async_computation | async-start | bytes 786432 | tf_op jit(solution)/shard_map/all_to_all | solution.py:78
  55.9 6.7 %all-to-all-done = bf16[192,8,128]{2,0,1:T(8,128)(2,1)S(1)} async-done(((bf16[192,8,128]{2,0,1:T(8,128)(2,1)}), bf16[192,8,128]{2,0,1:T(8,128)(2,1)S(1)}, u32[]{:S(2)}, u32[]{:S(2)}) %all-to-all-start) | async-done | bytes 393248 | tf_op jit(solution)/shard_map/all_to_all | solution.py:78
  63.6 29.1 %while.39 = (s32[]{:T(128)}, f32[2,1536,128]{2,1,0:T(8,128)}, f32[3,512,1,128]{3,1,2,0:T(8,128)}, s32[3,512]{1,0:T(4,128)}, s32[1536]{0:T(1024)S(1)}, /*index=5*...) while((s32[]{:T(128)}, f32[2,1536,128]{2,1,0:T(8,128)}, ...), condition=%wide.region_3.4_spmd.clone, body=%wide.region_2.3_spmd.clone.sunk | while | flops 1016467968 | bytes 28805472 | solution.py:64
  69.9 2.4 fusion.153
  77.4 2.8 maximum_add_fusion.6
  80.1 2.4 fusion.153
  87.6 2.8 maximum_add_fusion.6
  96.6 3.8 %collective-permute-start.1 = (bf16[2,1536,128]{2,1,0:T(8,128)(2,1)}, bf16[2,1536,128]{2,1,0:T(8,128)(2,1)}, u32[]{:S(2)}, u32[]{:S(2)}) collective-permute-start(bf16[2,1536,128]{2,1,0:T(8,128)(2,1)} %collective-permute-done), channel_id=1, source_target_pairs={{0,1},{1,2},{2,3},{3,4},{4,5},{5,6},{6,7},{7,8},{8,9},{9,10},{10,1... | collective-permute-start | bytes 2359304 | tf_op jit(solution)/shard_map/ppermute | solution.py:14
  101.4 29.0 %while.40 = (s32[]{:T(128)}, f32[2,1536,128]{2,1,0:T(8,128)}, f32[3,512,1,128]{3,1,2,0:T(8,128)}, s32[3,512]{1,0:T(4,128)}, s32[1536]{0:T(1024)S(1)}, /*index=5*...) while((s32[]{:T(128)}, f32[2,1536,128]{2,1,0:T(8,128)}, ...), condition=%wide.region_6.7_spmd.clone, body=%wide.region_5.6_spmd.clone.sunk | while | flops 1016467968 | bytes 28780876 | solution.py:64
  107.7 2.4 fusion.166
  115.2 2.7 maximum_add_fusion.7
  117.9 2.4 fusion.166
  125.3 2.7 maximum_add_fusion.7
  128.1 2.3 fusion.166
  130.4 17.8 %collective-permute-done.1 = bf16[2,1536,128]{2,1,0:T(8,128)(2,1)} collective-permute-done((bf16[2,1536,128]{2,1,0:T(8,128)(2,1)}, bf16[2,1536,128]{2,1,0:T(8,128)(2,1)}, u32[]{:S(2)}, u32[]{:S(2)}) %collective-permute-start.1) | collective-permute-done | bytes 786464 | tf_op jit(solution)/shard_map/ppermute | solution.py:14
  150.2 2.7 add.100
  153.9 29.0 %while.41 = (s32[]{:T(128)}, f32[2,1536,128]{2,1,0:T(8,128)}, f32[3,512,1,128]{3,1,2,0:T(8,128)}, s32[3,512]{1,0:T(4,128)}, s32[1536]{0:T(1024)S(1)}, /*index=5*...) while((s32[]{:T(128)}, f32[2,1536,128]{2,1,0:T(8,128)}, ...), condition=%wide.region_9.10_spmd.clone, body=%wide.region_8.9_spmd.clone.sunk | while | flops 1016467968 | bytes 28780876 | solution.py:64
  160.2 2.3 fusion.179
  167.6 2.7 maximum_add_fusion.8
  170.4 2.3 fusion.179
  177.8 2.7 maximum_add_fusion.8
  180.5 2.3 fusion.179
  182.9 7.9 %collective-permute-done.3 = f32[2,1536,128]{2,1,0:T(8,128)} collective-permute-done((f32[2,1536,128]{2,1,0:T(8,128)}, f32[2,1536,128]{2,1,0:T(8,128)}, u32[]{:S(2)}, u32[]{:S(2)}) %collective-permute-start.3) | collective-permute-done | bytes 1572896 | tf_op jit(solution)/shard_map/ppermute | solution.py:20
  193.6 66.4 %collective-permute-done.4 = f32[2,1536,128]{2,1,0:T(8,128)S(1)} collective-permute-done((f32[2,1536,128]{2,1,0:T(8,128)S(1)}, f32[2,1536,128]{2,1,0:T(8,128)S(1)}, u32[]{:S(2)}, u32[]{:S(2)}) %collective-permute-start.4) | collective-permute-done | bytes 1572896 | tf_op jit(solution)/shard_map/ppermute | solution.py:20
  264.5 12.3 %all_to_all.63 = bf16[8,2,12288]{2,1,0:T(2,128)(2,1)S(1)} all-to-all(bf16[8,2,12288]{2,1,0:T(2,128)(2,1)S(1)} %reshape.625), channel_id=1, replica_groups=mesh['ulysses'=8,'blk'=32] {'ulysses'}, dimensions={0} | all-to-all | bytes 786432 | tf_op jit(solution)/shard_map/all_to_all | solution.py:106
  278.3 18.0 %reduce-scatter.2.cloned.1.call-done = f32[2,192,128]{2,1,0:T(8,128)} async-done(((f32[2,1536,128]{2,1,0:T(8,128)}), f32[2,192,128]{2,1,0:T(8,128)}) %reduce-scatter.2.cloned.1.call-update) | async-done | bytes 196624 | tf_op jit(solution)/shard_map/reduce_scatter | solution.py:103
  (232 shorter events, 80.6 us)
Async XLA Ops:
  7.2 25.4 %copy-start.14 = (bf16[192,8,128]{2,1,0:T(8,128)(2,1)S(1)}, bf16[192,8,128]{2,1,0:T(8,128)(2,1)}, u32[]{:S(2)}) copy-start(bf16[192,8,128]{2,1,0:T(8,128)(2,1)} %param.17) | copy-start | bytes 1179652
  7.2 21.1 %copy-start.22 = (f32[8,192]{1,0:T(8,128)S(1)}, f32[8,192]{1,0:T(8,128)}, u32[]{:S(2)}) copy-start(f32[8,192]{1,0:T(8,128)} %param.18) | copy-start | bytes 18436
  7.2 26.2 %copy-start.23 = (s32[32]{0:T(128)S(1)}, s32[32]{0:T(128)}, u32[]{:S(2)}) copy-start(s32[32]{0:T(128)} %param.19) | copy-start | bytes 388
  7.2 26.5 %copy-start.15 = (bf16[192,8,128]{2,1,0:T(8,128)(2,1)S(1)}, bf16[192,8,128]{2,1,0:T(8,128)(2,1)}, u32[]{:S(2)}) copy-start(bf16[192,8,128]{2,1,0:T(8,128)(2,1)} %param.13) | copy-start | bytes 1179652
  22.9 71.8 %collective-permute-start = (bf16[2,1536,128]{2,1,0:T(8,128)(2,1)}, bf16[2,1536,128]{2,1,0:T(8,128)(2,1)}, u32[]{:S(2)}, u32[]{:S(2)}) collective-permute-start(bf16[2,1536,128]{2,1,0:T(8,128)(2,1)} %all_gather.3), channel_id=1, source_target_pairs={{0,1},{1,2},{2,3},{3,4},{4,5},{5,6},{6,7},{7,8},{8,9},{9,10},{10,1... | collective-permute-start | bytes 2359304 | tf_op jit(solution)/shard_map/ppermute | solution.py:14
  28.9 9.0 %all-to-all-start.1 = ((f32[2,192,8]{1,0,2:T(2,128)}), f32[2,192,8]{1,0,2:T(2,128)S(1)}, u32[]{:S(2)}, u32[]{:S(2)}) async-start(f32[2,192,8]{1,0,2:T(2,128)} %pad_maximum_fusion.1), calls=%async_computation.1 | async-start | bytes 32768 | tf_op jit(solution)/shard_map/all_to_all | solution.py:74
  37.9 12.3 %all-to-all-start.2 = ((bf16[192,8,128]{2,0,1:T(8,128)(2,1)}), bf16[192,8,128]{2,0,1:T(8,128)(2,1)S(1)}, u32[]{:S(2)}, u32[]{:S(2)}) async-start(bf16[192,8,128]{2,0,1:T(8,128)(2,1)} %copy.61), calls=%async_computation.2 | async-start | bytes 786432 | tf_op jit(solution)/shard_map/all_to_all | solution.py:79
  50.3 12.3 %all-to-all-start = ((bf16[192,8,128]{2,0,1:T(8,128)(2,1)}), bf16[192,8,128]{2,0,1:T(8,128)(2,1)S(1)}, u32[]{:S(2)}, u32[]{:S(2)}) async-start(bf16[192,8,128]{2,0,1:T(8,128)(2,1)} %copy.60), calls=%async_computation | async-start | bytes 786432 | tf_op jit(solution)/shard_map/all_to_all | solution.py:78
  53.7 242.5 %reduce-scatter.2.cloned.1.call-start = ((), (), s32[]{:S(2)}) async-start(), calls=%async_computation.5 | async-start | bytes 1769472 | tf_op jit(solution)/shard_map/reduce_scatter | solution.py:103
  63.6 3.8 %copy-start.7 = (bf16[3,512,1,128]{3,1,2,0:T(8,128)(2,1)}, bf16[3,512,1,128]{3,1,2,0:T(8,128)(2,1)S(1)}, u32[]{:S(2)}) copy-start(bf16[3,512,1,128]{3,1,2,0:T(8,128)(2,1)S(1)} %get-tuple-element.1006) | copy-start | bytes 1179652 | tf_op jit(solution)/shard_map/while
  72.3 3.2 %copy-start.16 = (s32[1536]{0:T(1024)}, s32[1536]{0:T(1024)S(1)}, u32[]{:S(2)}) copy-start(s32[1536]{0:T(1024)S(1)} %get-tuple-element.1004) | copy-start | bytes 18436 | tf_op jit(solution)/shard_map/while
  72.3 3.2 %copy-start.1 = (bf16[1536,128]{1,0:T(8,128)(2,1)}, bf16[1536,128]{1,0:T(8,128)(2,1)S(1)}, u32[]{:S(2)}) copy-start(bf16[1536,128]{1,0:T(8,128)(2,1)S(1)} %get-tuple-element.1010) | copy-start | bytes 1179652 | tf_op jit(solution)/shard_map/while
  72.3 3.8 %copy-start.7 = (bf16[3,512,1,128]{3,1,2,0:T(8,128)(2,1)}, bf16[3,512,1,128]{3,1,2,0:T(8,128)(2,1)S(1)}, u32[]{:S(2)}) copy-start(bf16[3,512,1,128]{3,1,2,0:T(8,128)(2,1)S(1)} %get-tuple-element.1006) | copy-start | bytes 1179652 | tf_op jit(solution)/shard_map/while
  82.5 3.2 %copy-start.16 = (s32[1536]{0:T(1024)}, s32[1536]{0:T(1024)S(1)}, u32[]{:S(2)}) copy-start(s32[1536]{0:T(1024)S(1)} %get-tuple-element.1004) | copy-start | bytes 18436 | tf_op jit(solution)/shard_map/while
  82.5 3.2 %copy-start.1 = (bf16[1536,128]{1,0:T(8,128)(2,1)}, bf16[1536,128]{1,0:T(8,128)(2,1)S(1)}, u32[]{:S(2)}) copy-start(bf16[1536,128]{1,0:T(8,128)(2,1)S(1)} %get-tuple-element.1010) | copy-start | bytes 1179652 | tf_op jit(solution)/shard_map/while
  82.5 3.8 %copy-start.7 = (bf16[3,512,1,128]{3,1,2,0:T(8,128)(2,1)}, bf16[3,512,1,128]{3,1,2,0:T(8,128)(2,1)S(1)}, u32[]{:S(2)}) copy-start(bf16[3,512,1,128]{3,1,2,0:T(8,128)(2,1)S(1)} %get-tuple-element.1006) | copy-start | bytes 1179652 | tf_op jit(solution)/shard_map/while
  92.7 8.8 %copy-start.20 = (s32[1536]{0:T(1024)S(1)}, s32[1536]{0:T(1024)}, u32[]{:S(2)}) copy-start(s32[1536]{0:T(1024)} %get-tuple-element.929) | copy-start | bytes 18436
  92.7 57.5 %collective-permute-start.2 = (f32[2,1536,128]{2,1,0:T(8,128)}, f32[2,1536,128]{2,1,0:T(8,128)}, u32[]{:S(2)}, u32[]{:S(2)}) collective-permute-start(f32[2,1536,128]{2,1,0:T(8,128)} %get-tuple-element.210), channel_id=1, source_target_pairs={{0,1},{1,2},{2,3},{3,4},{4,5},{5,6},{6,7},{7,8},{8,9},{9,10},{10,1... | collective-permute-start | bytes 4718600 | tf_op jit(solution)/shard_map/ppermute | solution.py:20
  96.6 51.7 %collective-permute-start.1 = (bf16[2,1536,128]{2,1,0:T(8,128)(2,1)}, bf16[2,1536,128]{2,1,0:T(8,128)(2,1)}, u32[]{:S(2)}, u32[]{:S(2)}) collective-permute-start(bf16[2,1536,128]{2,1,0:T(8,128)(2,1)} %collective-permute-done), channel_id=1, source_target_pairs={{0,1},{1,2},{2,3},{3,4},{4,5},{5,6},{6,7},{7,8},{8,9},{9,10},{10,1... | collective-permute-start | bytes 2359304 | tf_op jit(solution)/shard_map/ppermute | solution.py:14
  101.4 3.7 %copy-start.9 = (bf16[3,512,1,128]{3,1,2,0:T(8,128)(2,1)}, bf16[3,512,1,128]{3,1,2,0:T(8,128)(2,1)S(1)}, u32[]{:S(2)}) copy-start(bf16[3,512,1,128]{3,1,2,0:T(8,128)(2,1)S(1)} %get-tuple-element.961) | copy-start | bytes 1179652 | tf_op jit(solution)/shard_map/while
  110.1 3.2 %copy-start.5 = (bf16[1536,128]{1,0:T(8,128)(2,1)}, bf16[1536,128]{1,0:T(8,128)(2,1)S(1)}, u32[]{:S(2)}) copy-start(bf16[1536,128]{1,0:T(8,128)(2,1)S(1)} %get-tuple-element.965) | copy-start | bytes 1179652 | tf_op jit(solution)/shard_map/while
  110.2 3.8 %copy-start.9 = (bf16[3,512,1,128]{3,1,2,0:T(8,128)(2,1)}, bf16[3,512,1,128]{3,1,2,0:T(8,128)(2,1)S(1)}, u32[]{:S(2)}) copy-start(bf16[3,512,1,128]{3,1,2,0:T(8,128)(2,1)S(1)} %get-tuple-element.961) | copy-start | bytes 1179652 | tf_op jit(solution)/shard_map/while
  120.3 3.2 %copy-start.5 = (bf16[1536,128]{1,0:T(8,128)(2,1)}, bf16[1536,128]{1,0:T(8,128)(2,1)S(1)}, u32[]{:S(2)}) copy-start(bf16[1536,128]{1,0:T(8,128)(2,1)S(1)} %get-tuple-element.965) | copy-start | bytes 1179652 | tf_op jit(solution)/shard_map/while
  120.3 3.8 %copy-start.9 = (bf16[3,512,1,128]{3,1,2,0:T(8,128)(2,1)}, bf16[3,512,1,128]{3,1,2,0:T(8,128)(2,1)S(1)}, u32[]{:S(2)}) copy-start(bf16[3,512,1,128]{3,1,2,0:T(8,128)(2,1)S(1)} %get-tuple-element.961) | copy-start | bytes 1179652 | tf_op jit(solution)/shard_map/while
  130.4 19.8 %copy-start = (f32[2,1536,128]{2,1,0:T(8,128)S(1)}, f32[2,1536,128]{2,1,0:T(8,128)}, u32[]{:S(2)}) copy-start(f32[2,1536,128]{2,1,0:T(8,128)} %get-tuple-element.1054) | copy-start | bytes 4718596
  150.2 3.7 %copy-start.18 = (s32[1536]{0:T(1024)S(1)}, s32[1536]{0:T(1024)}, u32[]{:S(2)}) copy-start(s32[1536]{0:T(1024)} %get-tuple-element.884) | copy-start | bytes 18436
  152.9 37.8 %collective-permute-start.3 = (f32[2,1536,128]{2,1,0:T(8,128)}, f32[2,1536,128]{2,1,0:T(8,128)}, u32[]{:S(2)}, u32[]{:S(2)}) collective-permute-start(f32[2,1536,128]{2,1,0:T(8,128)} %add.100), channel_id=1, source_target_pairs={{0,1},{1,2},{2,3},{3,4},{4,5},{5,6},{6,7},{7,8},{8,9},{9,10},{10,1... | collective-permute-start | bytes 4718600 | tf_op jit(solution)/shard_map/ppermute | solution.py:20
  153.9 3.7 %copy-start.11 = (bf16[3,512,1,128]{3,1,2,0:T(8,128)(2,1)}, bf16[3,512,1,128]{3,1,2,0:T(8,128)(2,1)S(1)}, u32[]{:S(2)}) copy-start(bf16[3,512,1,128]{3,1,2,0:T(8,128)(2,1)S(1)} %get-tuple-element.916) | copy-start | bytes 1179652 | tf_op jit(solution)/shard_map/while
  162.6 3.8 %copy-start.11 = (bf16[3,512,1,128]{3,1,2,0:T(8,128)(2,1)}, bf16[3,512,1,128]{3,1,2,0:T(8,128)(2,1)S(1)}, u32[]{:S(2)}) copy-start(bf16[3,512,1,128]{3,1,2,0:T(8,128)(2,1)S(1)} %get-tuple-element.916) | copy-start | bytes 1179652 | tf_op jit(solution)/shard_map/while
  172.7 3.2 %copy-start.3 = (bf16[1536,128]{1,0:T(8,128)(2,1)}, bf16[1536,128]{1,0:T(8,128)(2,1)S(1)}, u32[]{:S(2)}) copy-start(bf16[1536,128]{1,0:T(8,128)(2,1)S(1)} %get-tuple-element.920) | copy-start | bytes 1179652 | tf_op jit(solution)/shard_map/while
  172.7 3.8 %copy-start.11 = (bf16[3,512,1,128]{3,1,2,0:T(8,128)(2,1)}, bf16[3,512,1,128]{3,1,2,0:T(8,128)(2,1)S(1)}, u32[]{:S(2)}) copy-start(bf16[3,512,1,128]{3,1,2,0:T(8,128)(2,1)S(1)} %get-tuple-element.916) | copy-start | bytes 1179652 | tf_op jit(solution)/shard_map/while
  192.8 67.3 %collective-permute-start.4 = (f32[2,1536,128]{2,1,0:T(8,128)S(1)}, f32[2,1536,128]{2,1,0:T(8,128)S(1)}, u32[]{:S(2)}, u32[]{:S(2)}) collective-permute-start(f32[2,1536,128]{2,1,0:T(8,128)S(1)} %add.101), channel_id=1, source_target_pairs={{0,30},{1,31},{2,0},{3,1},{4,2},{5,3},{6,4},{7,5},{8,6},{9,7},{10,... | collective-permute-start | bytes 4718600 | tf_op jit(solution)/shard_map/ppermute | solution.py:20
  (33 other events, 80.7 us)
Sparse Core Ops, SparseCore 0:
  261.4 34.8 reduce-scatter.1
where the time goes:
time: 308 us; the launch traced here: 306 us
  waiting for transfers between devices  127 us (41%)
  matrix products  58.2 us (19%)
  other arithmetic  34 us (11%)
  blocking collectives  27.1 us (9%)
  local copies, waits for them, and re-layouts  23.6 us (8%)
  starting transfers between devices  21.1 us (7%)
  between operations  14.2 us (5%)
    ppermute x3, waiting for transfers between devices, from_behind(): return lax.ppermute(value, axis, pairs)  74.3 us
    dot_general x9, matrix products, one(): jnp.einsum('hqk,kd->qhd', dscores, key_rows, preferred_element_type=jnp.f...  21.2 us
    dot_general x9, matrix products, one(): jnp.einsum('qhd,kd->hqk', qpart, key_rows, preferred_element_type=jnp.flo...  20.7 us
    add x9, other arithmetic, one(): return (carry + jnp.stack([dk_term, dv_term]), dq_part)  20.4 us
    reduce_scatter x1, waiting for transfers between devices, per_device(): total = lax.psum_scatter(total, 'ulysses', scatter_dimension=1, tiled=True)  18 us
    ppermute x2, waiting for transfers between devices, shifted(): return lax.ppermute(block, axis, route)  17.8 us
    all_gather x1, blocking collectives, per_device(): kv_local = lax.all_gather(kv_own, 'ulysses', axis=1, tiled=True)  14.8 us
    all_to_all x1, blocking collectives, per_device(): lax.all_to_all((dq_sum * scale).astype(jnp.bfloat16), 'ulysses', split_ax...  12.3 us
  transfers between devices with their start and end apart: 9, of which 7 were waited for; matrix products, arithmetic and copies ran while one was open for 35% of the time, Pallas kernels for 0%

commit v1 on v0

v1 whole, which is shorter than its diff:
```python
import math

import jax
import jax.numpy as jnp
from jax import lax
from jax.experimental import pallas as pl
from jax.experimental.pallas import tpu as pltpu
from jax.sharding import PartitionSpec as P

f32 = jnp.float32
bf16 = jnp.bfloat16
MESH = pl.DeviceIdType.MESH

HEADS = 8
WIDTH = 128
TOKENS = 192
ROWS = TOKENS * HEADS
GROUPS = 8
BLOCK = TOKENS * GROUPS
BLOCKS = 32
CHIPS = 4
NDOCS = 32
KEYS = 4 * TOKENS
HALF = ROWS // 2
SCALE = WIDTH ** -0.5
RATE = SCALE * math.log2(math.e)
FAR = float(2 ** 17)
LSE_LANE = NDOCS
FEATURES = NDOCS + 3 * HEADS

Z_IN = 0
X_IN = 2
C_IN = 8
C_OUT = 16
X_OUT = 24
Z_OUT = 30
MESSAGES = 32


def dot(a, b, ca, cb):
    return lax.dot_general(a, b, (((ca,), (cb,)), ((), ())), preferred_element_type=f32)


def three_parts(value):
    high = value.astype(bf16).astype(f32)
    middle = (value - high).astype(bf16).astype(f32)
    return high, middle, value - high - middle


def slot_of(dx, old, other):
    return dx * 4 + old * 2 + other


def kernel(
    len_ref, q_ref, k_ref, v_ref, o_ref, do_ref, lse_ref,
    dq_ref, dk_ref, dv_ref,
    own, slots, qx, dox, q_t, do_t, kx, vx, dq_acc, dk_acc, dv_acc, lse_pad,
    diag, part, c_in, x_out, x_in, z_out, z_in, send_sem, recv_sem,
):
    block = lax.axis_index("blk")
    index = lax.axis_index("ulysses")
    x = index // 2
    core = lax.rem(index, 2)

    def column(d):
        return {"blk": block, "ulysses": lax.rem(x + d, CHIPS) * 2 + core}

    def behind(steps):
        return {"blk": lax.rem(block + steps + BLOCKS, BLOCKS), "ulysses": index}

    partner = {"blk": block, "ulysses": x * 2 + 1 - core}

    barrier = pltpu.get_barrier_semaphore()
    others = [partner] + [column(d) for d in (1, 2, 3)] + [behind(s) for s in (1, 2, -1, -2)]
    for device in others:
        pl.semaphore_signal(barrier, inc=1, device_id=device, device_id_type=MESH)

    def message(number, source, target, device):
        return pltpu.make_async_remote_copy(
            src_ref=source,
            dst_ref=target,
            send_sem=send_sem.at[number],
            recv_sem=recv_sem.at[number],
            device_id=device,
            device_id_type=MESH,
        )

    def arrived(number):
        message(number, own, z_in.at[0], partner).wait_recv()

    lane = lax.broadcasted_iota(jnp.int32, (1, WIDTH), 1)
    starts = jnp.zeros((1, WIDTH), jnp.int32)
    ends = jnp.zeros((1, WIDTH), jnp.int32)
    for d in range(NDOCS):
        length = len_ref[d]
        starts = starts + jnp.where(lane > d, length, 0)
        ends = ends + jnp.where(lane >= d, length, 0)

    def in_doc(first):
        position = first + lax.broadcasted_iota(jnp.int32, (TOKENS, WIDTH), 0)
        return (position >= starts) & (position < ends)

    lanes = lax.broadcasted_iota(jnp.int32, (TOKENS, WIDTH), 1)

    def key_features(first):
        flag = jnp.where((lanes >= LSE_LANE) & (lanes < FEATURES), 1.0, 0.0)
        return jnp.where(in_doc(first), 1.0, flag).astype(bf16)

    here = block * BLOCK + index * TOKENS

    own[:, :WIDTH] = k_ref[...]
    own[:, WIDTH:] = v_ref[...]

    lse_pad[...] = jnp.zeros_like(lse_pad)
    for i, piece in enumerate(three_parts(lse_ref[...] * (-1.0 / SCALE))):
        lse_pad[LSE_LANE + i * HEADS : LSE_LANE + (i + 1) * HEADS, :TOKENS] = piece
    by_token = lse_pad[...].T[:TOKENS, :]
    by_token = jnp.where(lanes < NDOCS, jnp.where(in_doc(here), 0.0, -FAR), by_token)
    head = lax.broadcasted_iota(jnp.int32, (HEADS, WIDTH), 0)
    head_lane = lax.broadcasted_iota(jnp.int32, (HEADS, WIDTH), 1)
    chosen = jnp.where((head_lane < NDOCS) | (lax.rem(head_lane, HEADS) == head), 1.0, 0.0)
    qx[:, :WIDTH] = q_ref[...]
    qx[:, WIDTH:] = (by_token[:, None, :] * chosen[None]).reshape(ROWS, WIDTH).astype(bf16)

    douts = do_ref[...]
    delta = jnp.sum(douts.astype(f32) * o_ref[...].astype(f32), axis=1, keepdims=True)
    high, middle, low = three_parts(-delta)
    row_lane = lax.broadcasted_iota(jnp.int32, (ROWS, WIDTH), 1)
    dox[:, :WIDTH] = douts
    dox[:, WIDTH:] = jnp.where(
        row_lane == 0, high, jnp.where(row_lane == 1, middle, jnp.where(row_lane == 2, low, 0.0))
    ).astype(bf16)
    q_t[...] = q_ref[...].T
    do_t[...] = douts.T
    key_lane = lax.broadcasted_iota(jnp.int32, (KEYS, WIDTH), 1)
    vx[:, WIDTH:] = jnp.where(key_lane < 3, 1.0, 0.0).astype(bf16)

    def half(i, keys, values, mask):
        rows = pl.ds(i * HALF, HALF)
        probs = jnp.exp2(dot(qx[rows, :], keys, 1, 1) * RATE)
        if mask is not None:
            probs = jnp.where(mask, probs, 0.0)
        dscores = (probs * dot(dox[rows, :], values, 1, 1)).astype(bf16)
        probs = probs.astype(bf16)
        dq = dot(dscores, keys[:, :WIDTH], 1, 0)
        dk = dot(q_t[:, rows], dscores, 1, 0)
        dv = dot(do_t[:, rows], probs, 1, 0)
        return dq, dk, dv

    own_keys = jnp.concatenate([k_ref[...], key_features(here)], axis=1)
    own_values = jnp.concatenate([v_ref[...], vx[:TOKENS, WIDTH:]], axis=1)
    dk_sum, dv_sum = 0.0, 0.0
    for i in range(2):
        token = lax.broadcasted_iota(jnp.int32, (HALF, TOKENS), 0) // HEADS + i * (HALF // HEADS)
        mask = lax.broadcasted_iota(jnp.int32, (HALF, TOKENS), 1) <= token
        dq, dk, dv = half(i, own_keys, own_values, mask)
        dq_acc[i * HALF : (i + 1) * HALF, :] = dq
        dk_sum, dv_sum = dk_sum + dk, dv_sum + dv
    diag[:, :WIDTH] = dk_sum.T
    diag[:, WIDTH:] = dv_sum.T

    pl.semaphore_wait(barrier, len(others))

    message(Z_IN, own, slots.at[slot_of(0, 0, 0)], behind(1)).start()
    message(Z_IN + 1, own, slots.at[slot_of(0, 1, 0)], behind(2)).start()

    def along_x(d, old, source):
        r = CHIPS - d
        message(
            X_IN + (r - 1) * 2 + old, source, slots.at[slot_of(r, old, 0)], column(d)
        ).start()

    def across(dx, old, source):
        message(C_IN + dx * 2 + old, source, slots.at[slot_of(dx, old, 1)], partner).start()

    for d in (1, 3, 2):
        @pl.when(x + d < CHIPS)
        def _():
            along_x(d, 1, own)

    @pl.when(core == 0)
    def _():
        across(0, 1, own)

    arrived(Z_IN)
    for d in (1, 3, 2):
        along_x(d, 0, slots.at[slot_of(0, 0, 0)])
    across(0, 0, slots.at[slot_of(0, 0, 0)])
    arrived(Z_IN + 1)
    for d in (1, 3, 2):
        @pl.when(x + d >= CHIPS)
        def _():
            along_x(d, 1, slots.at[slot_of(0, 1, 0)])

    @pl.when(core == 1)
    def _():
        across(0, 1, slots.at[slot_of(0, 1, 0)])

    def pass_on(dx, old):
        arrived(X_IN + (dx - 1) * 2 + old)
        across(dx, old, slots.at[slot_of(dx, old, 0)])

    def first_of(dx, old, other):
        from_x = lax.rem(x + dx, CHIPS)
        from_core = (1 - core) if other else core
        from_index = from_x * 2 + from_core
        if old == 0:
            back = 1
        else:
            back = jnp.where(from_index < index, 0, 2)
        return lax.rem(block - back + BLOCKS, BLOCKS) * BLOCK + from_index * TOKENS

    def assemble(pairs):
        for i, (dx, old) in enumerate(pairs):
            arrived(C_IN + dx * 2 + old)
            for other in range(2):
                rows = slice((i * 2 + other) * TOKENS, (i * 2 + other + 1) * TOKENS)
                slot = slot_of(dx, old, other)
                kx[rows, :WIDTH] = slots[slot, :, :WIDTH]
                kx[rows, WIDTH:] = key_features(first_of(dx, old, other))
                vx[rows, :WIDTH] = slots[slot, :, WIDTH:]

    def compute(i):
        dq, dk, dv = half(i, kx[...], vx[...], None)
        dq_acc[i * HALF : (i + 1) * HALF, :] += dq
        if i == 0:
            dk_acc[...] = dk
            dv_acc[...] = dv
        else:
            dk_acc[...] += dk
            dv_acc[...] += dv

    def give(pairs):
        dk = dk_acc[...].T.astype(bf16)
        dv = dv_acc[...].T.astype(bf16)
        for i, (dx, old) in enumerate(pairs):
            for other in range(2):
                rows = slice((i * 2 + other) * TOKENS, (i * 2 + other + 1) * TOKENS)
                part[slot_of(dx, old, other), :, :WIDTH] = dk[rows]
                part[slot_of(dx, old, other), :, WIDTH:] = dv[rows]
            message(
                C_OUT + dx * 2 + old, part.at[slot_of(dx, old, 1)], c_in.at[dx * 2 + old], partner
            ).start()

    def combine(dx, old):
        arrived(C_OUT + dx * 2 + old)
        place = (dx - 1) * 2 + old
        total = part[slot_of(dx, old, 0)].astype(f32) + c_in[dx * 2 + old].astype(f32)
        x_out[place] = total.astype(bf16)
        r = CHIPS - dx
        number = (r - 1) * 2 + old
        message(X_OUT + number, x_out.at[place], x_in.at[number], column(dx)).start()

    def taken(flag, value):
        return jnp.where(flag, value.astype(f32), 0.0)

    order = [
        [(1, 0), (3, 0)],
        [(1, 1), (3, 1)],
        [(0, 1), (2, 1)],
        [(0, 0), (2, 0)],
    ]
    pass_on(1, 0)
    pass_on(3, 0)
    assemble(order[0])
    compute(0)
    pass_on(1, 1)
    pass_on(3, 1)
    pass_on(2, 0)
    compute(1)
    give(order[0])
    pass_on(2, 1)
    assemble(order[1])
    compute(0)
    combine(1, 0)
    combine(3, 0)
    compute(1)
    give(order[1])
    assemble(order[2])
    compute(0)
    combine(1, 1)
    combine(3, 1)
    compute(1)
    give(order[2])
    assemble(order[3])
    compute(0)
    combine(2, 1)
    compute(1)
    give(order[3])

    for d in (1, 2, 3):
        arrived(X_OUT + (d - 1) * 2 + 1)
    arrived(C_OUT + 1)
    later = part[slot_of(0, 1, 0)].astype(f32) + taken(core == 1, c_in[1])
    for d in (1, 2, 3):
        later = later + taken(x + d >= CHIPS, x_in[(d - 1) * 2 + 1])
    z_out[1] = later.astype(bf16)
    message(Z_OUT + 1, z_out.at[1], z_in.at[1], behind(-2)).start()
    combine(2, 0)
    mine = diag[...] + taken(core == 0, c_in[1])
    for d in (1, 2, 3):
        mine = mine + taken(x + d < CHIPS, x_in[(d - 1) * 2 + 1])
    diag[...] = mine
    dq_ref[...] = (dq_acc[...] * SCALE).astype(bf16)
    arrived(C_OUT)
    total = part[slot_of(0, 0, 0)].astype(f32) + c_in[0].astype(f32)
    for d in (1, 3, 2):
        arrived(X_OUT + (d - 1) * 2)
        total = total + x_in[(d - 1) * 2].astype(f32)
    z_out[0] = total.astype(bf16)
    message(Z_OUT, z_out.at[0], z_in.at[0], behind(-1)).start()
    arrived(Z_OUT + 1)
    arrived(Z_OUT)
    mine = diag[...] + z_in[0].astype(f32) + z_in[1].astype(f32)
    dk_ref[...] = (mine[:, :WIDTH] * SCALE).astype(bf16)
    dv_ref[...] = mine[:, WIDTH:].astype(bf16)
    for number in range(MESSAGES):
        message(number, own, z_in.at[0], partner).wait_send()


def per_device(query, key, value, output, grad_out, lse, doc_lengths):
    vmem = pl.BlockSpec(memory_space=pltpu.VMEM)
    chunk = (TOKENS, 2 * WIDTH)
    dq, dk, dv = pl.pallas_call(
        kernel,
        out_shape=(
            jax.ShapeDtypeStruct((ROWS, WIDTH), bf16),
            jax.ShapeDtypeStruct((TOKENS, WIDTH), bf16),
            jax.ShapeDtypeStruct((TOKENS, WIDTH), bf16),
        ),
        in_specs=[pl.BlockSpec(memory_space=pltpu.SMEM)] + [vmem] * 6,
        out_specs=(vmem, vmem, vmem),
        scratch_shapes=[
            pltpu.VMEM(chunk, bf16),
            pltpu.VMEM((16,) + chunk, bf16),
            pltpu.VMEM((ROWS, 2 * WIDTH), bf16),
            pltpu.VMEM((ROWS, 2 * WIDTH), bf16),
            pltpu.VMEM((WIDTH, ROWS), bf16),
            pltpu.VMEM((WIDTH, ROWS), bf16),
            pltpu.VMEM((KEYS, 2 * WIDTH), bf16),
            pltpu.VMEM((KEYS, 2 * WIDTH), bf16),
            pltpu.VMEM((ROWS, WIDTH), f32),
            pltpu.VMEM((WIDTH, KEYS), f32),
            pltpu.VMEM((WIDTH, KEYS), f32),
            pltpu.VMEM((WIDTH, 2 * WIDTH), f32),
            pltpu.VMEM(chunk, f32),
            pltpu.VMEM((16,) + chunk, bf16),
            pltpu.VMEM((8,) + chunk, bf16),
            pltpu.VMEM((6,) + chunk, bf16),
            pltpu.VMEM((6,) + chunk, bf16),
            pltpu.VMEM((2,) + chunk, bf16),
            pltpu.VMEM((2,) + chunk, bf16),
            pltpu.SemaphoreType.DMA((MESSAGES,)),
            pltpu.SemaphoreType.DMA((MESSAGES,)),
        ],
        compiler_params=pltpu.CompilerParams(
            collective_id=0, has_side_effects=True, vmem_limit_bytes=56 * 2**20
        ),
    )(
        doc_lengths,
        query.reshape(ROWS, WIDTH),
        key,
        value,
        output.reshape(ROWS, WIDTH),
        grad_out.reshape(ROWS, WIDTH),
        lse,
    )
    return (dq.reshape(TOKENS, HEADS, WIDTH), dk, dv)


def solution(mesh):
    tokens = P(("blk", "ulysses"), None, None)
    rows = P(("blk", "ulysses"), None)
    return jax.shard_map(
        per_device,
        mesh=mesh,
        in_specs=(tokens, rows, rows, tokens, tokens, P(None, ("blk", "ulysses")), P()),
        out_specs=(tokens, rows, rows),
        check_vma=False,
    )
```

time: 308 us -> 56.2 us (0.18)
  the two profiles are of different devices: /device:TPU:24 before, /device:TPU:1 now
where the time goes in v1:
time: 56.2 us; the launch traced here: 56.1 us
  Pallas kernels  52.2 us (93%)
  local copies, waits for them, and re-layouts  3.22 us (6%)
  between operations  0.65 us (1%)
    pallas_call x1, Pallas kernels, per_device(): pl.pallas_call(kernel, out_shape=(jax.ShapeDtypeStruct((ROWS, WIDTH), bf1...  52.2 us
    unnamed x7, local copies, waits for them, and re-layouts  3.22 us

profile of v1, /device:TPU:1, one launch (start us, length us, event | category | flops | bytes accessed | tf_op | source)
XLA Modules:
  0.0 56.1 jit_solution(1347740000486467186)
XLA Ops:
  0.6 52.2 %shard_map.94 = (bf16[1536,128]{1,0:T(8,128)(2,1)}, bf16[192,128]{1,0:T(8,128)(2,1)}, bf16[192,128]{1,0:T(8,128)(2,1)}) custom-call(s32[32]{0:T(128)} %len_ref.1, bf16[1536,128]{1,0:T(8,128)(2,1)} %bitcast.5, bf16[192,128]{1,0:T(8,128)(2,1)} %k_ref.1, bf16[192,128]{1,0:T(8,128)(2,1)} %v_ref.1, bf16[1536,128]{1,0:T(8,128)(2,1)} %bitcast.6, ...), custom_call_target="tpu_custom_call" | custom-call | tf_op jit(solution)/shard_map/pallas_call | solution.py:324
  52.8 0.0 copy-start.1
  52.8 1.8 %copy.13 = bf16[192,8,128]{2,1,0:T(8,128)(2,1)} copy(bf16[192,8,128]{2,1,0:T(8,128)(2,1)} %bitcast.4) | data formatting | bytes 786432
  54.6 0.0 copy-done.1
  54.6 0.0 copy-start
  54.6 0.6 %copy.14 = bf16[192,128]{1,0:T(8,128)(2,1)} copy(bf16[192,128]{1,0:T(8,128)(2,1)S(1)} %copy-done.1) | data formatting | bytes 98304
  55.2 0.2 copy-done
  55.4 0.6 %copy.15 = bf16[192,128]{1,0:T(8,128)(2,1)} copy(bf16[192,128]{1,0:T(8,128)(2,1)S(1)} %copy-done) | data formatting | bytes 98304
Async XLA Ops:
  52.8 1.8 %copy-start.1 = (bf16[192,128]{1,0:T(8,128)(2,1)S(1)}, bf16[192,128]{1,0:T(8,128)(2,1)}, u32[]{:S(2)}) copy-start(bf16[192,128]{1,0:T(8,128)(2,1)} %get-tuple-element.13) | copy-start | bytes 147460
  54.6 0.8 %copy-start = (bf16[192,128]{1,0:T(8,128)(2,1)S(1)}, bf16[192,128]{1,0:T(8,128)(2,1)}, u32[]{:S(2)}) copy-start(bf16[192,128]{1,0:T(8,128)(2,1)} %get-tuple-element.14) | copy-start | bytes 147460

commit v2 on v1

--- a/solution.py
+++ b/solution.py
@@ -54,8 +54,8 @@
 def kernel(
     len_ref, q_ref, k_ref, v_ref, o_ref, do_ref, lse_ref,
     dq_ref, dk_ref, dv_ref,
-    own, slots, qx, dox, q_t, do_t, kx, vx, dq_acc, dk_acc, dv_acc, lse_pad,
-    diag, part, c_in, x_out, x_in, z_out, z_in, send_sem, recv_sem,
+    own, slots, qx, dox, q_t, do_t, outs, lse_in, kx, vx, dq_acc, dk_acc, dv_acc, lse_pad,
+    diag, part, c_in, x_out, x_in, z_out, z_in, result, send_sem, recv_sem, load_sem, store_sem,
 ):
     block = lax.axis_index("blk")
     index = lax.axis_index("ulysses")
@@ -70,10 +70,32 @@
 
     partner = {"blk": block, "ulysses": x * 2 + 1 - core}
 
+    def exists(steps):
+        return (block + steps >= 0) & (block + steps < BLOCKS)
+
     barrier = pltpu.get_barrier_semaphore()
-    others = [partner] + [column(d) for d in (1, 2, 3)] + [behind(s) for s in (1, 2, -1, -2)]
-    for device in others:
+    for device in [partner] + [column(d) for d in (1, 2, 3)]:
         pl.semaphore_signal(barrier, inc=1, device_id=device, device_id_type=MESH)
+    greeted = 4
+    for steps in (2, -2, 1, -1):
+        @pl.when(exists(steps))
+        def _():
+            pl.semaphore_signal(barrier, inc=1, device_id=behind(steps), device_id_type=MESH)
+        greeted = greeted + jnp.where(exists(steps), 1, 0)
+
+    loads = [
+        pltpu.make_async_copy(source, target, load_sem.at[i])
+        for i, (source, target) in enumerate([
+            (k_ref, own.at[:, :WIDTH]),
+            (v_ref, own.at[:, WIDTH:]),
+            (lse_ref, lse_in),
+            (do_ref, dox.at[:, :WIDTH]),
+            (o_ref, outs),
+            (q_ref, qx.at[:, :WIDTH]),
+        ])
+    ]
+    for load in loads:
+        load.start()
 
     def message(number, source, target, device):
         return pltpu.make_async_remote_copy(
@@ -88,6 +110,37 @@
     def arrived(number):
         message(number, own, z_in.at[0], partner).wait_recv()
 
+    def along_x(d, old, source):
+        r = CHIPS - d
+        message(
+            X_IN + (r - 1) * 2 + old, source, slots.at[slot_of(r, old, 0)], column(d)
+        ).start()
+
+    def across(dx, old, source):
+        message(C_IN + dx * 2 + old, source, slots.at[slot_of(dx, old, 1)], partner).start()
+
+    loads[0].wait()
+    loads[1].wait()
+    pl.semaphore_wait(barrier, greeted)
+    for steps in (1, 2):
+        @pl.when(exists(steps))
+        def _():
+            target = slots.at[slot_of(0, steps - 1, 0)]
+            message(Z_IN + steps - 1, own, target, behind(steps)).start()
+
+        @pl.when(~exists(-steps))
+        def _():
+            slots[slot_of(0, steps - 1, 0)] = jnp.zeros((TOKENS, 2 * WIDTH), bf16)
+
+    for d in (1, 3, 2):
+        @pl.when(x + d < CHIPS)
+        def _():
+            along_x(d, 1, own)
+
+    @pl.when(core == 0)
+    def _():
+        across(0, 1, own)
+
     lane = lax.broadcasted_iota(jnp.int32, (1, WIDTH), 1)
     starts = jnp.zeros((1, WIDTH), jnp.int32)
     ends = jnp.zeros((1, WIDTH), jnp.int32)
@@ -108,30 +161,29 @@
 
     here = block * BLOCK + index * TOKENS
 
-    own[:, :WIDTH] = k_ref[...]
-    own[:, WIDTH:] = v_ref[...]
-
+    loads[2].wait()
     lse_pad[...] = jnp.zeros_like(lse_pad)
-    for i, piece in enumerate(three_parts(lse_ref[...] * (-1.0 / SCALE))):
+    for i, piece in enumerate(three_parts(lse_in[...] * (-1.0 / SCALE))):
         lse_pad[LSE_LANE + i * HEADS : LSE_LANE + (i + 1) * HEADS, :TOKENS] = piece
     by_token = lse_pad[...].T[:TOKENS, :]
     by_token = jnp.where(lanes < NDOCS, jnp.where(in_doc(here), 0.0, -FAR), by_token)
     head = lax.broadcasted_iota(jnp.int32, (HEADS, WIDTH), 0)
     head_lane = lax.broadcasted_iota(jnp.int32, (HEADS, WIDTH), 1)
     chosen = jnp.where((head_lane < NDOCS) | (lax.rem(head_lane, HEADS) == head), 1.0, 0.0)
-    qx[:, :WIDTH] = q_ref[...]
     qx[:, WIDTH:] = (by_token[:, None, :] * chosen[None]).reshape(ROWS, WIDTH).astype(bf16)
 
-    douts = do_ref[...]
-    delta = jnp.sum(douts.astype(f32) * o_ref[...].astype(f32), axis=1, keepdims=True)
+    loads[3].wait()
+    loads[4].wait()
+    douts = dox[:, :WIDTH]
+    delta = jnp.sum(douts.astype(f32) * outs[...].astype(f32), axis=1, keepdims=True)
     high, middle, low = three_parts(-delta)
     row_lane = lax.broadcasted_iota(jnp.int32, (ROWS, WIDTH), 1)
-    dox[:, :WIDTH] = douts
     dox[:, WIDTH:] = jnp.where(
         row_lane == 0, high, jnp.where(row_lane == 1, middle, jnp.where(row_lane == 2, low, 0.0))
     ).astype(bf16)
-    q_t[...] = q_ref[...].T
     do_t[...] = douts.T
+    loads[5].wait()
+    q_t[...] = qx[:, :WIDTH].T
     key_lane = lax.broadcasted_iota(jnp.int32, (KEYS, WIDTH), 1)
     vx[:, WIDTH:] = jnp.where(key_lane < 3, 1.0, 0.0).astype(bf16)
 
@@ -147,8 +199,16 @@
         dv = dot(do_t[:, rows], probs, 1, 0)
         return dq, dk, dv
 
-    own_keys = jnp.concatenate([k_ref[...], key_features(here)], axis=1)
-    own_values = jnp.concatenate([v_ref[...], vx[:TOKENS, WIDTH:]], axis=1)
+    @pl.when(exists(-1))
+    def _():
+        arrived(Z_IN)
+
+    for d in (1, 3, 2):
+        along_x(d, 0, slots.at[slot_of(0, 0, 0)])
+    across(0, 0, slots.at[slot_of(0, 0, 0)])
+
+    own_keys = jnp.concatenate([own[:, :WIDTH], key_features(here)], axis=1)
+    own_values = jnp.concatenate([own[:, WIDTH:], vx[:TOKENS, WIDTH:]], axis=1)
     dk_sum, dv_sum = 0.0, 0.0
     for i in range(2):
         token = lax.broadcasted_iota(jnp.int32, (HALF, TOKENS), 0) // HEADS + i * (HALF // HEADS)
@@ -159,43 +219,6 @@
     diag[:, :WIDTH] = dk_sum.T
     diag[:, WIDTH:] = dv_sum.T
 
-    pl.semaphore_wait(barrier, len(others))
-
-    message(Z_IN, own, slots.at[slot_of(0, 0, 0)], behind(1)).start()
-    message(Z_IN + 1, own, slots.at[slot_of(0, 1, 0)], behind(2)).start()
-
-    def along_x(d, old, source):
-        r = CHIPS - d
-        message(
-            X_IN + (r - 1) * 2 + old, source, slots.at[slot_of(r, old, 0)], column(d)
-        ).start()
-
-    def across(dx, old, source):
-        message(C_IN + dx * 2 + old, source, slots.at[slot_of(dx, old, 1)], partner).start()
-
-    for d in (1, 3, 2):
-        @pl.when(x + d < CHIPS)
-        def _():
-            along_x(d, 1, own)
-
-    @pl.when(core == 0)
-    def _():
-        across(0, 1, own)
-
-    arrived(Z_IN)
-    for d in (1, 3, 2):
-        along_x(d, 0, slots.at[slot_of(0, 0, 0)])
-    across(0, 0, slots.at[slot_of(0, 0, 0)])
-    arrived(Z_IN + 1)
-    for d in (1, 3, 2):
-        @pl.when(x + d >= CHIPS)
-        def _():
-            along_x(d, 1, slots.at[slot_of(0, 1, 0)])
-
-    @pl.when(core == 1)
-    def _():
-        across(0, 1, slots.at[slot_of(0, 1, 0)])
-
     def pass_on(dx, old):
         arrived(X_IN + (dx - 1) * 2 + old)
         across(dx, old, slots.at[slot_of(dx, old, 0)])
@@ -220,19 +243,21 @@
                 kx[rows, WIDTH:] = key_features(first_of(dx, old, other))
                 vx[rows, :WIDTH] = slots[slot, :, WIDTH:]
 
-    def compute(i):
-        dq, dk, dv = half(i, kx[...], vx[...], None)
+    def compute(pairs, i):
+        keys = len(pairs) * 2 * TOKENS
+        dq, dk, dv = half(i, kx[:keys, :], vx[:keys, :], None)
         dq_acc[i * HALF : (i + 1) * HALF, :] += dq
         if i == 0:
-            dk_acc[...] = dk
-            dv_acc[...] = dv
+            dk_acc[:, :keys] = dk
+            dv_acc[:, :keys] = dv
         else:
-            dk_acc[...] += dk
-            dv_acc[...] += dv
+            dk_acc[:, :keys] += dk
+            dv_acc[:, :keys] += dv
 
     def give(pairs):
-        dk = dk_acc[...].T.astype(bf16)
-        dv = dv_acc[...].T.astype(bf16)
+        keys = len(pairs) * 2 * TOKENS
+        dk = dk_acc[:, :keys].T.astype(bf16)
+        dv = dv_acc[:, :keys].T.astype(bf16)
         for i, (dx, old) in enumerate(pairs):
             for other in range(2):
                 rows = slice((i * 2 + other) * TOKENS, (i * 2 + other + 1) * TOKENS)
@@ -254,82 +279,140 @@
     def taken(flag, value):
         return jnp.where(flag, value.astype(f32), 0.0)
 
-    order = [
-        [(1, 0), (3, 0)],
-        [(1, 1), (3, 1)],
-        [(0, 1), (2, 1)],
-        [(0, 0), (2, 0)],
-    ]
+    first = [(0, 0)]
+    assemble(first)
+    compute(first, 0)
+    compute(first, 1)
+    give(first)
+
+    @pl.when(exists(-2))
+    def _():
+        arrived(Z_IN + 1)
+
+    for d in (1, 3, 2):
+        @pl.when(x + d >= CHIPS)
+        def _():
+            along_x(d, 1, slots.at[slot_of(0, 1, 0)])
+
+    @pl.when(core == 1)
+    def _():
+        across(0, 1, slots.at[slot_of(0, 1, 0)])
+
     pass_on(1, 0)
     pass_on(3, 0)
-    assemble(order[0])
-    compute(0)
+    group = [(1, 0), (3, 0)]
+    assemble(group)
+    compute(group, 0)
+    pass_on(2, 0)
+    compute(group, 1)
+    give(group)
     pass_on(1, 1)
     pass_on(3, 1)
-    pass_on(2, 0)
-    compute(1)
-    give(order[0])
+    group = [(2, 0), (0, 1)]
+    assemble(group)
+    compute(group, 0)
     pass_on(2, 1)
-    assemble(order[1])
-    compute(0)
     combine(1, 0)
     combine(3, 0)
-    compute(1)
-    give(order[1])
-    assemble(order[2])
-    compute(0)
+    compute(group, 1)
+    give(group)
+    group = [(1, 1), (3, 1)]
+    assemble(group)
+    compute(group, 0)
+    combine(2, 0)
+    compute(group, 1)
+    give(group)
+    group = [(2, 1)]
+    assemble(group)
+    compute(group, 0)
     combine(1, 1)
     combine(3, 1)
-    compute(1)
-    give(order[2])
-    assemble(order[3])
-    compute(0)
+    compute(group, 1)
+    give(group)
     combine(2, 1)
-    compute(1)
-    give(order[3])
-
-    for d in (1, 2, 3):
-        arrived(X_OUT + (d - 1) * 2 + 1)
-    arrived(C_OUT + 1)
-    later = part[slot_of(0, 1, 0)].astype(f32) + taken(core == 1, c_in[1])
-    for d in (1, 2, 3):
-        later = later + taken(x + d >= CHIPS, x_in[(d - 1) * 2 + 1])
-    z_out[1] = later.astype(bf16)
-    message(Z_OUT + 1, z_out.at[1], z_in.at[1], behind(-2)).start()
-    combine(2, 0)
-    mine = diag[...] + taken(core == 0, c_in[1])
-    for d in (1, 2, 3):
-        mine = mine + taken(x + d < CHIPS, x_in[(d - 1) * 2 + 1])
-    diag[...] = mine
-    dq_ref[...] = (dq_acc[...] * SCALE).astype(bf16)
+
+    result[...] = (dq_acc[...] * SCALE).astype(bf16)
+    store = pltpu.make_async_copy(result, dq_ref, store_sem.at[0])
+    store.start()
     arrived(C_OUT)
     total = part[slot_of(0, 0, 0)].astype(f32) + c_in[0].astype(f32)
     for d in (1, 3, 2):
         arrived(X_OUT + (d - 1) * 2)
         total = total + x_in[(d - 1) * 2].astype(f32)
     z_out[0] = total.astype(bf16)
-    message(Z_OUT, z_out.at[0], z_in.at[0], behind(-1)).start()
-    arrived(Z_OUT + 1)
-    arrived(Z_OUT)
-    mine = diag[...] + z_in[0].astype(f32) + z_in[1].astype(f32)
-    dk_ref[...] = (mine[:, :WIDTH] * SCALE).astype(bf16)
-    dv_ref[...] = mine[:, WIDTH:].astype(bf16)
-    for number in range(MESSAGES):
+
+    @pl.when(exists(-1))
+    def _():
+        message(Z_OUT, z_out.at[0], z_in.at[0], behind(-1)).start()
+
+    arrived(C_OUT + 1)
+    later = part[slot_of(0, 1, 0)].astype(f32) + taken(core == 1, c_in[1])
+    mine = diag[...] + taken(core == 0, c_in[1])
+    for d in (1, 3, 2):
+        arrived(X_OUT + (d - 1) * 2 + 1)
+        later = later + taken(x + d >= CHIPS, x_in[(d - 1) * 2 + 1])
+        mine = mine + taken(x + d < CHIPS, x_in[(d - 1) * 2 + 1])
+    z_out[1] = later.astype(bf16)
+
+    @pl.when(exists(-2))
+    def _():
+        message(Z_OUT + 1, z_out.at[1], z_in.at[1], behind(-2)).start()
+
+    diag[...] = mine
+    for steps in (1, 2):
+        @pl.when(exists(steps))
+        def _():
+            arrived(Z_OUT + steps - 1)
+            diag[...] += z_in[steps - 1].astype(f32)
+
+    outs[:TOKENS, :] = (diag[:, :WIDTH] * SCALE).astype(bf16)
+    outs[TOKENS : 2 * TOKENS, :] = diag[:, WIDTH:].astype(bf16)
+    last = [
+        pltpu.make_async_copy(outs.at[:TOKENS], dk_ref, store_sem.at[1]),
+        pltpu.make_async_copy(outs.at[TOKENS : 2 * TOKENS], dv_ref, store_sem.at[2]),
+    ]
+    for copy in last:
+        copy.start()
+    for copy in [store] + last:
+        copy.wait()
+    for number in range(X_IN, Z_OUT):
         message(number, own, z_in.at[0], partner).wait_send()
+    for steps in (1, 2):
+        @pl.when(exists(steps))
+        def _():
+            message(Z_IN + steps - 1, own, z_in.at[0], partner).wait_send()
+
+        @pl.when(exists(-steps))
+        def _():
+            message(Z_OUT + steps - 1, own, z_in.at[0], partner).wait_send()
+
+
+def hand_over(dq_in, dk_in, dv_in, dq_out, dk_out, dv_out, sem):
+    copies = [
+        pltpu.make_async_copy(source, target, sem.at[i])
+        for i, (source, target) in enumerate(
+            [(dq_in, dq_out), (dk_in, dk_out), (dv_in, dv_out)]
+        )
+    ]
+    for copy in copies:
+        copy.start()
+    for copy in copies:
+        copy.wait()
 
 
 def per_device(query, key, value, output, grad_out, lse, doc_lengths):
-    vmem = pl.BlockSpec(memory_space=pltpu.VMEM)
+    anywhere = pl.BlockSpec(memory_space=pl.ANY)
     chunk = (TOKENS, 2 * WIDTH)
-    dq, dk, dv = pl.pallas_call(
+    shapes = (
+        jax.ShapeDtypeStruct((ROWS, WIDTH), bf16),
+        jax.ShapeDtypeStruct((TOKENS, WIDTH), bf16),
+        jax.ShapeDtypeStruct((TOKENS, WIDTH), bf16),
+    )
+    grads = pl.pallas_call(
         kernel,
-        out_shape=(
-            jax.ShapeDtypeStruct((ROWS, WIDTH), bf16),
-            jax.ShapeDtypeStruct((TOKENS, WIDTH), bf16),
-            jax.ShapeDtypeStruct((TOKENS, WIDTH), bf16),
-        ),
-        in_specs=[pl.BlockSpec(memory_space=pltpu.SMEM)] + [vmem] * 6,
-        out_specs=(vmem, vmem, vmem),
+        out_shape=shapes,
+        in_specs=[pl.BlockSpec(memory_space=pltpu.SMEM)] + [anywhere] * 6,
+        out_specs=(anywhere,) * 3,
         scratch_shapes=[
             pltpu.VMEM(chunk, bf16),
             pltpu.VMEM((16,) + chunk, bf16),
@@ -337,6 +420,8 @@
             pltpu.VMEM((ROWS, 2 * WIDTH), bf16),
             pltpu.VMEM((WIDTH, ROWS), bf16),
             pltpu.VMEM((WIDTH, ROWS), bf16),
+            pltpu.VMEM((ROWS, WIDTH), bf16),
+            pltpu.VMEM((HEADS, TOKENS), f32),
             pltpu.VMEM((KEYS, 2 * WIDTH), bf16),
             pltpu.VMEM((KEYS, 2 * WIDTH), bf16),
             pltpu.VMEM((ROWS, WIDTH), f32),
@@ -350,8 +435,11 @@
             pltpu.VMEM((6,) + chunk, bf16),
             pltpu.VMEM((2,) + chunk, bf16),
             pltpu.VMEM((2,) + chunk, bf16),
+            pltpu.VMEM((ROWS, WIDTH), bf16),
             pltpu.SemaphoreType.DMA((MESSAGES,)),
             pltpu.SemaphoreType.DMA((MESSAGES,)),
+            pltpu.SemaphoreType.DMA((6,)),
+            pltpu.SemaphoreType.DMA((3,)),
         ],
         compiler_params=pltpu.CompilerParams(
             collective_id=0, has_side_effects=True, vmem_limit_bytes=56 * 2**20
@@ -365,6 +453,13 @@
         grad_out.reshape(ROWS, WIDTH),
         lse,
     )
+    dq, dk, dv = pl.pallas_call(
+        hand_over,
+        out_shape=shapes,
+        in_specs=[anywhere] * 3,
+        out_specs=(anywhere,) * 3,
+        scratch_shapes=[pltpu.SemaphoreType.DMA((3,))],
+    )(*grads)
     return (dq.reshape(TOKENS, HEADS, WIDTH), dk, dv)
 
 

time: 56.2 us -> 62.9 us (1.12)
  the two profiles are of different devices: /device:TPU:1 before, /device:TPU:24 now
where the time goes in v2:
time: 62.9 us; the launch traced here: 62.7 us
  Pallas kernels  61.9 us (98%)
  between operations  0.8 us (1%)
    pallas_call x1, Pallas kernels, per_device(): pl.pallas_call(kernel, out_shape=shapes, in_specs=[pl.BlockSpec(memory_sp...  45.9 us
    pallas_call x1, Pallas kernels, per_device(): pl.pallas_call(hand_over, out_shape=shapes, in_specs=[anywhere] * 3, out_...  16 us

profile of v2, /device:TPU:24, one launch (start us, length us, event | category | flops | bytes accessed | tf_op | source)
XLA Modules:
  0.0 62.7 jit_solution(15653917661279085636)
XLA Ops:
  0.6 45.9 %shard_map.94 = (bf16[1536,128]{1,0:T(8,128)(2,1)}, bf16[192,128]{1,0:T(8,128)(2,1)}, bf16[192,128]{1,0:T(8,128)(2,1)}) custom-call(s32[32]{0:T(128)} %len_ref.1, bf16[1536,128]{1,0:T(8,128)(2,1)} %bitcast.4, bf16[192,128]{1,0:T(8,128)(2,1)} %k_ref.1, bf16[192,128]{1,0:T(8,128)(2,1)} %v_ref.1, bf16[1536,128]{1,0:T(8,128)(2,1)} %bitcast.5, ...), custom_call_target="tpu_custom_call" | custom-call | tf_op jit(solution)/shard_map/pallas_call | solution.py:411
  46.5 16.0 %shard_map.95 = (bf16[1536,128]{1,0:T(8,128)(2,1)}, bf16[192,128]{1,0:T(8,128)(2,1)}, bf16[192,128]{1,0:T(8,128)(2,1)}) custom-call(bf16[1536,128]{1,0:T(8,128)(2,1)} %get-tuple-element.9.dq_in, bf16[192,128]{1,0:T(8,128)(2,1)} %get-tuple-element.10.dk_in, bf16[192,128]{1,0:T(8,128)(2,1)} %get-tuple-element.11.dv_in), custom_call_target="tpu_custom_call" | custom-call | tf_op jit(solution)/shard_map/pallas_call | solution.py:456

commit v3 on v2

--- a/solution.py
+++ b/solution.py
@@ -35,6 +35,8 @@
 X_OUT = 24
 Z_OUT = 30
 MESSAGES = 32
+PIECES = 2
+PIECE = TOKENS // PIECES
 
 
 def dot(a, b, ca, cb):
@@ -97,37 +99,38 @@
     for load in loads:
         load.start()
 
-    def message(number, source, target, device):
+    def message(number, p, source, target, device):
+        rows = pl.ds(p * PIECE, PIECE)
         return pltpu.make_async_remote_copy(
-            src_ref=source,
-            dst_ref=target,
-            send_sem=send_sem.at[number],
-            recv_sem=recv_sem.at[number],
+            src_ref=source.at[rows],
+            dst_ref=target.at[rows],
+            send_sem=send_sem.at[number * PIECES + p],
+            recv_sem=recv_sem.at[number * PIECES + p],
             device_id=device,
             device_id_type=MESH,
         )
 
-    def arrived(number):
-        message(number, own, z_in.at[0], partner).wait_recv()
-
-    def along_x(d, old, source):
+    def arrived(number, p):
+        message(number, p, own, z_in.at[0], partner).wait_recv()
+
+    def along_x(d, old, p, source):
         r = CHIPS - d
         message(
-            X_IN + (r - 1) * 2 + old, source, slots.at[slot_of(r, old, 0)], column(d)
+            X_IN + (r - 1) * 2 + old, p, source, slots.at[slot_of(r, old, 0)], column(d)
         ).start()
 
-    def across(dx, old, source):
-        message(C_IN + dx * 2 + old, source, slots.at[slot_of(dx, old, 1)], partner).start()
+    def across(dx, old, p, source):
+        message(C_IN + dx * 2 + old, p, source, slots.at[slot_of(dx, old, 1)], partner).start()
 
     loads[0].wait()
     loads[1].wait()
     pl.semaphore_wait(barrier, greeted)
+    @pl.when(exists(1))
+    def _():
+        for p in range(PIECES):
+            message(Z_IN, p, own, slots.at[slot_of(0, 0, 0)], behind(1)).start()
+
     for steps in (1, 2):
-        @pl.when(exists(steps))
-        def _():
-            target = slots.at[slot_of(0, steps - 1, 0)]
-            message(Z_IN + steps - 1, own, target, behind(steps)).start()
-
         @pl.when(~exists(-steps))
         def _():
             slots[slot_of(0, steps - 1, 0)] = jnp.zeros((TOKENS, 2 * WIDTH), bf16)
@@ -135,11 +138,13 @@
     for d in (1, 3, 2):
         @pl.when(x + d < CHIPS)
         def _():
-            along_x(d, 1, own)
+            for p in range(PIECES):
+                along_x(d, 1, p, own)
 
     @pl.when(core == 0)
     def _():
-        across(0, 1, own)
+        for p in range(PIECES):
+            across(0, 1, p, own)
 
     lane = lax.broadcasted_iota(jnp.int32, (1, WIDTH), 1)
     starts = jnp.zeros((1, WIDTH), jnp.int32)
@@ -199,13 +204,19 @@
         dv = dot(do_t[:, rows], probs, 1, 0)
         return dq, dk, dv
 
-    @pl.when(exists(-1))
-    def _():
-        arrived(Z_IN)
-
-    for d in (1, 3, 2):
-        along_x(d, 0, slots.at[slot_of(0, 0, 0)])
-    across(0, 0, slots.at[slot_of(0, 0, 0)])
+    before = slots.at[slot_of(0, 0, 0)]
+    for p in range(PIECES):
+        @pl.when(exists(-1))
+        def _():
+            arrived(Z_IN, p)
+
+            @pl.when(exists(1))
+            def _():
+                message(Z_IN + 1, p, before, slots.at[slot_of(0, 1, 0)], behind(1)).start()
+
+        for d in (1, 3, 2):
+            along_x(d, 0, p, before)
+        across(0, 0, p, before)
 
     own_keys = jnp.concatenate([own[:, :WIDTH], key_features(here)], axis=1)
     own_values = jnp.concatenate([own[:, WIDTH:], vx[:TOKENS, WIDTH:]], axis=1)
@@ -220,8 +231,9 @@
     diag[:, WIDTH:] = dv_sum.T
 
     def pass_on(dx, old):
-        arrived(X_IN + (dx - 1) * 2 + old)
-        across(dx, old, slots.at[slot_of(dx, old, 0)])
+        for p in range(PIECES):
+            arrived(X_IN + (dx - 1) * 2 + old, p)
+            across(dx, old, p, slots.at[slot_of(dx, old, 0)])
 
     def first_of(dx, old, other):
         from_x = lax.rem(x + dx, CHIPS)
@@ -235,7 +247,8 @@
 
     def assemble(pairs):
         for i, (dx, old) in enumerate(pairs):
-            arrived(C_IN + dx * 2 + old)
+            for p in range(PIECES):
+                arrived(C_IN + dx * 2 + old, p)
             for other in range(2):
                 rows = slice((i * 2 + other) * TOKENS, (i * 2 + other + 1) * TOKENS)
                 slot = slot_of(dx, old, other)
@@ -263,18 +276,21 @@
                 rows = slice((i * 2 + other) * TOKENS, (i * 2 + other + 1) * TOKENS)
                 part[slot_of(dx, old, other), :, :WIDTH] = dk[rows]
                 part[slot_of(dx, old, other), :, WIDTH:] = dv[rows]
-            message(
-                C_OUT + dx * 2 + old, part.at[slot_of(dx, old, 1)], c_in.at[dx * 2 + old], partner
-            ).start()
+            for p in range(PIECES):
+                message(
+                    C_OUT + dx * 2 + old, p, part.at[slot_of(dx, old, 1)], c_in.at[dx * 2 + old],
+                    partner,
+                ).start()
 
     def combine(dx, old):
-        arrived(C_OUT + dx * 2 + old)
         place = (dx - 1) * 2 + old
-        total = part[slot_of(dx, old, 0)].astype(f32) + c_in[dx * 2 + old].astype(f32)
-        x_out[place] = total.astype(bf16)
-        r = CHIPS - dx
-        number = (r - 1) * 2 + old
-        message(X_OUT + number, x_out.at[place], x_in.at[number], column(dx)).start()
+        number = (CHIPS - dx - 1) * 2 + old
+        for p in range(PIECES):
+            rows = slice(p * PIECE, (p + 1) * PIECE)
+            arrived(C_OUT + dx * 2 + old, p)
+            total = part[slot_of(dx, old, 0), rows].astype(f32) + c_in[dx * 2 + old, rows].astype(f32)
+            x_out[place, rows] = total.astype(bf16)
+            message(X_OUT + number, p, x_out.at[place], x_in.at[number], column(dx)).start()
 
     def taken(flag, value):
         return jnp.where(flag, value.astype(f32), 0.0)
@@ -285,18 +301,20 @@
     compute(first, 1)
     give(first)
 
-    @pl.when(exists(-2))
-    def _():
-        arrived(Z_IN + 1)
-
-    for d in (1, 3, 2):
-        @pl.when(x + d >= CHIPS)
-        def _():
-            along_x(d, 1, slots.at[slot_of(0, 1, 0)])
-
-    @pl.when(core == 1)
-    def _():
-        across(0, 1, slots.at[slot_of(0, 1, 0)])
+    before_that = slots.at[slot_of(0, 1, 0)]
+    for p in range(PIECES):
+        @pl.when(exists(-2))
+        def _():
+            arrived(Z_IN + 1, p)
+
+        for d in (1, 3, 2):
+            @pl.when(x + d >= CHIPS)
+            def _():
+                along_x(d, 1, p, before_that)
+
+        @pl.when(core == 1)
+        def _():
+            across(0, 1, p, before_that)
 
     pass_on(1, 0)
     pass_on(3, 0)
@@ -308,7 +326,7 @@
     give(group)
     pass_on(1, 1)
     pass_on(3, 1)
-    group = [(2, 0), (0, 1)]
+    group = [(1, 1), (3, 1)]
     assemble(group)
     compute(group, 0)
     pass_on(2, 1)
@@ -316,54 +334,61 @@
     combine(3, 0)
     compute(group, 1)
     give(group)
-    group = [(1, 1), (3, 1)]
-    assemble(group)
-    compute(group, 0)
-    combine(2, 0)
-    compute(group, 1)
-    give(group)
-    group = [(2, 1)]
+    group = [(2, 1), (0, 1)]
     assemble(group)
     compute(group, 0)
     combine(1, 1)
     combine(3, 1)
     compute(group, 1)
     give(group)
+    group = [(2, 0)]
+    assemble(group)
+    compute(group, 0)
     combine(2, 1)
+    compute(group, 1)
+    give(group)
+    combine(2, 0)
 
     result[...] = (dq_acc[...] * SCALE).astype(bf16)
     store = pltpu.make_async_copy(result, dq_ref, store_sem.at[0])
     store.start()
-    arrived(C_OUT)
-    total = part[slot_of(0, 0, 0)].astype(f32) + c_in[0].astype(f32)
-    for d in (1, 3, 2):
-        arrived(X_OUT + (d - 1) * 2)
-        total = total + x_in[(d - 1) * 2].astype(f32)
-    z_out[0] = total.astype(bf16)
-
-    @pl.when(exists(-1))
-    def _():
-        message(Z_OUT, z_out.at[0], z_in.at[0], behind(-1)).start()
-
-    arrived(C_OUT + 1)
-    later = part[slot_of(0, 1, 0)].astype(f32) + taken(core == 1, c_in[1])
-    mine = diag[...] + taken(core == 0, c_in[1])
-    for d in (1, 3, 2):
-        arrived(X_OUT + (d - 1) * 2 + 1)
-        later = later + taken(x + d >= CHIPS, x_in[(d - 1) * 2 + 1])
-        mine = mine + taken(x + d < CHIPS, x_in[(d - 1) * 2 + 1])
-    z_out[1] = later.astype(bf16)
-
-    @pl.when(exists(-2))
-    def _():
-        message(Z_OUT + 1, z_out.at[1], z_in.at[1], behind(-2)).start()
-
-    diag[...] = mine
-    for steps in (1, 2):
+    for p in range(PIECES):
+        rows = slice(p * PIECE, (p + 1) * PIECE)
+        arrived(C_OUT + 1, p)
+        later = part[slot_of(0, 1, 0), rows].astype(f32) + taken(core == 1, c_in[1, rows])
+        mine = diag[rows] + taken(core == 0, c_in[1, rows])
+        for d in (1, 3, 2):
+            arrived(X_OUT + (d - 1) * 2 + 1, p)
+            received = x_in[(d - 1) * 2 + 1, rows]
+            later = later + taken(x + d >= CHIPS, received)
+            mine = mine + taken(x + d < CHIPS, received)
+        z_out[1, rows] = later.astype(bf16)
+        diag[rows] = mine
+
+        @pl.when(exists(-2))
+        def _():
+            message(Z_OUT + 1, p, z_out.at[1], z_in.at[1], behind(-2)).start()
+
+    for p in range(PIECES):
+        rows = slice(p * PIECE, (p + 1) * PIECE)
+        arrived(C_OUT, p)
+        total = part[slot_of(0, 0, 0), rows].astype(f32) + c_in[0, rows].astype(f32)
+        for d in (1, 3, 2):
+            arrived(X_OUT + (d - 1) * 2, p)
+            total = total + x_in[(d - 1) * 2, rows].astype(f32)
+        z_out[0, rows] = total.astype(bf16)
+
+        @pl.when(exists(-1))
+        def _():
+            message(Z_OUT, p, z_out.at[0], z_in.at[0], behind(-1)).start()
+
+    for steps in (2, 1):
         @pl.when(exists(steps))
         def _():
-            arrived(Z_OUT + steps - 1)
-            diag[...] += z_in[steps - 1].astype(f32)
+            for p in range(PIECES):
+                rows = slice(p * PIECE, (p + 1) * PIECE)
+                arrived(Z_OUT + steps - 1, p)
+                diag[rows] += z_in[steps - 1, rows].astype(f32)
 
     outs[:TOKENS, :] = (diag[:, :WIDTH] * SCALE).astype(bf16)
     outs[TOKENS : 2 * TOKENS, :] = diag[:, WIDTH:].astype(bf16)
@@ -375,29 +400,27 @@
         copy.start()
     for copy in [store] + last:
         copy.wait()
+
+    def left(number):
+        for p in range(PIECES):
+            message(number, p, own, z_in.at[0], partner).wait_send()
+
     for number in range(X_IN, Z_OUT):
-        message(number, own, z_in.at[0], partner).wait_send()
+        left(number)
     for steps in (1, 2):
-        @pl.when(exists(steps))
-        def _():
-            message(Z_IN + steps - 1, own, z_in.at[0], partner).wait_send()
+        @pl.when(exists(1) & exists(1 - steps))
+        def _():
+            left(Z_IN + steps - 1)
 
         @pl.when(exists(-steps))
         def _():
-            message(Z_OUT + steps - 1, own, z_in.at[0], partner).wait_send()
-
-
-def hand_over(dq_in, dk_in, dv_in, dq_out, dk_out, dv_out, sem):
-    copies = [
-        pltpu.make_async_copy(source, target, sem.at[i])
-        for i, (source, target) in enumerate(
-            [(dq_in, dq_out), (dk_in, dk_out), (dv_in, dv_out)]
-        )
-    ]
-    for copy in copies:
-        copy.start()
-    for copy in copies:
-        copy.wait()
+            left(Z_OUT + steps - 1)
+
+
+def hand_over(dq_in, dk_in, dv_in, dq_out, dk_out, dv_out):
+    dq_out[...] = dq_in[...]
+    dk_out[...] = dk_in[...]
+    dv_out[...] = dv_in[...]
 
 
 def per_device(query, key, value, output, grad_out, lse, doc_lengths):
@@ -436,8 +459,8 @@
             pltpu.VMEM((2,) + chunk, bf16),
             pltpu.VMEM((2,) + chunk, bf16),
             pltpu.VMEM((ROWS, WIDTH), bf16),
-            pltpu.SemaphoreType.DMA((MESSAGES,)),
-            pltpu.SemaphoreType.DMA((MESSAGES,)),
+            pltpu.SemaphoreType.DMA((MESSAGES * PIECES,)),
+            pltpu.SemaphoreType.DMA((MESSAGES * PIECES,)),
             pltpu.SemaphoreType.DMA((6,)),
             pltpu.SemaphoreType.DMA((3,)),
         ],
@@ -456,9 +479,8 @@
     dq, dk, dv = pl.pallas_call(
         hand_over,
         out_shape=shapes,
-        in_specs=[anywhere] * 3,
-        out_specs=(anywhere,) * 3,
-        scratch_shapes=[pltpu.SemaphoreType.DMA((3,))],
+        in_specs=[pl.BlockSpec(memory_space=pltpu.VMEM)] * 3,
+        out_specs=(pl.BlockSpec(memory_space=pltpu.VMEM),) * 3,
     )(*grads)
     return (dq.reshape(TOKENS, HEADS, WIDTH), dk, dv)
 

time: 62.9 us -> 46.9 us (0.75)
  Pallas kernels: 61.9 us -> 46.1 us
    pallas_call x1, Pallas kernels: 16 us -> 1.81 us  [per_device(): pl.pallas_call(hand_over, out_shape=shapes, in_specs=[pl.BlockSpec(memory...]
    pallas_call x1, Pallas kernels: 45.9 us -> 44.3 us  [per_device(): pl.pallas_call(kernel, out_shape=shapes, in_specs=[pl.BlockSpec(memory_sp...]
where the time goes in v3:
time: 46.9 us; the launch traced here: 46.7 us
  Pallas kernels  46.1 us (98%)
  between operations  0.64 us (1%)
    pallas_call x1, Pallas kernels, per_device(): pl.pallas_call(kernel, out_shape=shapes, in_specs=[pl.BlockSpec(memory_sp...  44.3 us
    pallas_call x1, Pallas kernels, per_device(): pl.pallas_call(hand_over, out_shape=shapes, in_specs=[pl.BlockSpec(memory...  1.81 us

profile of v3, /device:TPU:24, one launch (start us, length us, event | category | flops | bytes accessed | tf_op | source)
XLA Modules:
  0.0 46.7 jit_solution(12553459689484205562)
XLA Ops:
  0.6 44.3 %shard_map.94 = (bf16[1536,128]{1,0:T(8,128)(2,1)}, bf16[192,128]{1,0:T(8,128)(2,1)}, bf16[192,128]{1,0:T(8,128)(2,1)}) custom-call(s32[32]{0:T(128)} %len_ref.1, bf16[1536,128]{1,0:T(8,128)(2,1)} %bitcast.4, bf16[192,128]{1,0:T(8,128)(2,1)} %k_ref.1, bf16[192,128]{1,0:T(8,128)(2,1)} %v_ref.1, bf16[1536,128]{1,0:T(8,128)(2,1)} %bitcast.5, ...), custom_call_target="tpu_custom_call" | custom-call | tf_op jit(solution)/shard_map/pallas_call | solution.py:434
  44.9 1.8 %shard_map.95 = (bf16[1536,128]{1,0:T(8,128)(2,1)}, bf16[192,128]{1,0:T(8,128)(2,1)}, bf16[192,128]{1,0:T(8,128)(2,1)}) custom-call(bf16[1536,128]{1,0:T(8,128)(2,1)} %get-tuple-element.9.dq_in, bf16[192,128]{1,0:T(8,128)(2,1)} %get-tuple-element.10.dk_in, bf16[192,128]{1,0:T(8,128)(2,1)} %get-tuple-element.11.dv_in), custom_call_target="tpu_custom_call" | custom-call | tf_op jit(solution)/shard_map/pallas_call | solution.py:479

commit v4 on v3

--- a/solution.py
+++ b/solution.py
@@ -35,8 +35,19 @@
 X_OUT = 24
 Z_OUT = 30
 MESSAGES = 32
-PIECES = 2
-PIECE = TOKENS // PIECES
+PIECES = {Z_IN: 2, X_IN: 2, C_IN: 2, C_OUT: 2, X_OUT: 2, Z_OUT: 2}
+MOST = 2
+
+
+def pieces(number):
+    return PIECES[max(first for first in PIECES if first <= number)]
+
+
+def within(number, p, other):
+    mine, its = pieces(number), pieces(other)
+    if its >= mine:
+        return range(p * its // mine, (p + 1) * its // mine)
+    return range(p * its // mine, p * its // mine + 1) if p % (mine // its) == 0 else range(0)
 
 
 def dot(a, b, ca, cb):
@@ -57,7 +68,7 @@
     len_ref, q_ref, k_ref, v_ref, o_ref, do_ref, lse_ref,
     dq_ref, dk_ref, dv_ref,
     own, slots, qx, dox, q_t, do_t, outs, lse_in, kx, vx, dq_acc, dk_acc, dv_acc, lse_pad,
-    diag, part, c_in, x_out, x_in, z_out, z_in, result, send_sem, recv_sem, load_sem, store_sem,
+    diag, total_acc, part, c_in, x_out, x_in, z_out, z_in, result, send_sem, recv_sem, load_sem, store_sem,
 ):
     block = lax.axis_index("blk")
     index = lax.axis_index("ulysses")
@@ -79,7 +90,7 @@
     for device in [partner] + [column(d) for d in (1, 2, 3)]:
         pl.semaphore_signal(barrier, inc=1, device_id=device, device_id_type=MESH)
     greeted = 4
-    for steps in (2, -2, 1, -1):
+    for steps in (1, -1):
         @pl.when(exists(steps))
         def _():
             pl.semaphore_signal(barrier, inc=1, device_id=behind(steps), device_id_type=MESH)
@@ -100,12 +111,13 @@
         load.start()
 
     def message(number, p, source, target, device):
-        rows = pl.ds(p * PIECE, PIECE)
+        size = TOKENS // pieces(number)
+        rows = pl.ds(p * size, size)
         return pltpu.make_async_remote_copy(
             src_ref=source.at[rows],
             dst_ref=target.at[rows],
-            send_sem=send_sem.at[number * PIECES + p],
-            recv_sem=recv_sem.at[number * PIECES + p],
+            send_sem=send_sem.at[number * MOST + p],
+            recv_sem=recv_sem.at[number * MOST + p],
             device_id=device,
             device_id_type=MESH,
         )
@@ -127,7 +139,7 @@
     pl.semaphore_wait(barrier, greeted)
     @pl.when(exists(1))
     def _():
-        for p in range(PIECES):
+        for p in range(pieces(Z_IN)):
             message(Z_IN, p, own, slots.at[slot_of(0, 0, 0)], behind(1)).start()
 
     for steps in (1, 2):
@@ -138,12 +150,12 @@
     for d in (1, 3, 2):
         @pl.when(x + d < CHIPS)
         def _():
-            for p in range(PIECES):
+            for p in range(pieces(X_IN)):
                 along_x(d, 1, p, own)
 
     @pl.when(core == 0)
     def _():
-        for p in range(PIECES):
+        for p in range(pieces(C_IN)):
             across(0, 1, p, own)
 
     lane = lax.broadcasted_iota(jnp.int32, (1, WIDTH), 1)
@@ -205,17 +217,19 @@
         return dq, dk, dv
 
     before = slots.at[slot_of(0, 0, 0)]
-    for p in range(PIECES):
+    for p in range(pieces(X_IN)):
         @pl.when(exists(-1))
         def _():
-            arrived(Z_IN, p)
-
-            @pl.when(exists(1))
-            def _():
-                message(Z_IN + 1, p, before, slots.at[slot_of(0, 1, 0)], behind(1)).start()
+            for q in within(X_IN, p, Z_IN):
+                arrived(Z_IN, q)
+
+                @pl.when(exists(1))
+                def _():
+                    message(Z_IN + 1, q, before, slots.at[slot_of(0, 1, 0)], behind(1)).start()
 
         for d in (1, 3, 2):
             along_x(d, 0, p, before)
+    for p in range(pieces(C_IN)):
         across(0, 0, p, before)
 
     own_keys = jnp.concatenate([own[:, :WIDTH], key_features(here)], axis=1)
@@ -231,8 +245,10 @@
     diag[:, WIDTH:] = dv_sum.T
 
     def pass_on(dx, old):
-        for p in range(PIECES):
-            arrived(X_IN + (dx - 1) * 2 + old, p)
+        came, goes = X_IN + (dx - 1) * 2 + old, C_IN + dx * 2 + old
+        for p in range(pieces(goes)):
+            for q in within(goes, p, came):
+                arrived(came, q)
             across(dx, old, p, slots.at[slot_of(dx, old, 0)])
 
     def first_of(dx, old, other):
@@ -247,7 +263,7 @@
 
     def assemble(pairs):
         for i, (dx, old) in enumerate(pairs):
-            for p in range(PIECES):
+            for p in range(pieces(C_IN)):
                 arrived(C_IN + dx * 2 + old, p)
             for other in range(2):
                 rows = slice((i * 2 + other) * TOKENS, (i * 2 + other + 1) * TOKENS)
@@ -269,14 +285,14 @@
 
     def give(pairs):
         keys = len(pairs) * 2 * TOKENS
-        dk = dk_acc[:, :keys].T.astype(bf16)
-        dv = dv_acc[:, :keys].T.astype(bf16)
+        dk = dk_acc[:, :keys].astype(bf16).T
+        dv = dv_acc[:, :keys].astype(bf16).T
         for i, (dx, old) in enumerate(pairs):
             for other in range(2):
                 rows = slice((i * 2 + other) * TOKENS, (i * 2 + other + 1) * TOKENS)
                 part[slot_of(dx, old, other), :, :WIDTH] = dk[rows]
                 part[slot_of(dx, old, other), :, WIDTH:] = dv[rows]
-            for p in range(PIECES):
+            for p in range(pieces(C_OUT)):
                 message(
                     C_OUT + dx * 2 + old, p, part.at[slot_of(dx, old, 1)], c_in.at[dx * 2 + old],
                     partner,
@@ -285,9 +301,11 @@
     def combine(dx, old):
         place = (dx - 1) * 2 + old
         number = (CHIPS - dx - 1) * 2 + old
-        for p in range(PIECES):
-            rows = slice(p * PIECE, (p + 1) * PIECE)
-            arrived(C_OUT + dx * 2 + old, p)
+        for p in range(pieces(X_OUT)):
+            size = TOKENS // pieces(X_OUT)
+            rows = slice(p * size, (p + 1) * size)
+            for q in within(X_OUT, p, C_OUT):
+                arrived(C_OUT + dx * 2 + old, q)
             total = part[slot_of(dx, old, 0), rows].astype(f32) + c_in[dx * 2 + old, rows].astype(f32)
             x_out[place, rows] = total.astype(bf16)
             message(X_OUT + number, p, x_out.at[place], x_in.at[number], column(dx)).start()
@@ -295,25 +313,26 @@
     def taken(flag, value):
         return jnp.where(flag, value.astype(f32), 0.0)
 
-    first = [(0, 0)]
-    assemble(first)
-    compute(first, 0)
-    compute(first, 1)
-    give(first)
-
+    group = [(0, 0)]
+    assemble(group)
+    compute(group, 0)
+    compute(group, 1)
+    give(group)
     before_that = slots.at[slot_of(0, 1, 0)]
-    for p in range(PIECES):
+    for p in range(pieces(X_IN)):
         @pl.when(exists(-2))
         def _():
-            arrived(Z_IN + 1, p)
-
-        for d in (1, 3, 2):
+            for q in within(X_IN, p, Z_IN + 1):
+                arrived(Z_IN + 1, q)
+
+        for d in (2, 1, 3):
             @pl.when(x + d >= CHIPS)
             def _():
                 along_x(d, 1, p, before_that)
 
-        @pl.when(core == 1)
-        def _():
+    @pl.when(core == 1)
+    def _():
+        for p in range(pieces(C_IN)):
             across(0, 1, p, before_that)
 
     pass_on(1, 0)
@@ -325,26 +344,26 @@
     compute(group, 1)
     give(group)
     pass_on(1, 1)
-    pass_on(3, 1)
-    group = [(1, 1), (3, 1)]
+    pass_on(2, 1)
+    group = [(1, 1), (2, 1)]
     assemble(group)
     compute(group, 0)
-    pass_on(2, 1)
+    pass_on(3, 1)
     combine(1, 0)
     combine(3, 0)
     compute(group, 1)
     give(group)
-    group = [(2, 1), (0, 1)]
+    group = [(3, 1), (0, 1)]
     assemble(group)
     compute(group, 0)
+    combine(2, 1)
     combine(1, 1)
-    combine(3, 1)
     compute(group, 1)
     give(group)
     group = [(2, 0)]
     assemble(group)
     compute(group, 0)
-    combine(2, 1)
+    combine(3, 1)
     compute(group, 1)
     give(group)
     combine(2, 0)
@@ -352,13 +371,16 @@
     result[...] = (dq_acc[...] * SCALE).astype(bf16)
     store = pltpu.make_async_copy(result, dq_ref, store_sem.at[0])
     store.start()
-    for p in range(PIECES):
-        rows = slice(p * PIECE, (p + 1) * PIECE)
-        arrived(C_OUT + 1, p)
+    size = TOKENS // pieces(Z_OUT)
+    for p in range(pieces(Z_OUT)):
+        rows = slice(p * size, (p + 1) * size)
+        for q in within(Z_OUT, p, C_OUT):
+            arrived(C_OUT + 1, q)
         later = part[slot_of(0, 1, 0), rows].astype(f32) + taken(core == 1, c_in[1, rows])
         mine = diag[rows] + taken(core == 0, c_in[1, rows])
         for d in (1, 3, 2):
-            arrived(X_OUT + (d - 1) * 2 + 1, p)
+            for q in within(Z_OUT, p, X_OUT):
+                arrived(X_OUT + (d - 1) * 2 + 1, q)
             received = x_in[(d - 1) * 2 + 1, rows]
             later = later + taken(x + d >= CHIPS, received)
             mine = mine + taken(x + d < CHIPS, received)
@@ -367,28 +389,47 @@
 
         @pl.when(exists(-2))
         def _():
-            message(Z_OUT + 1, p, z_out.at[1], z_in.at[1], behind(-2)).start()
-
-    for p in range(PIECES):
-        rows = slice(p * PIECE, (p + 1) * PIECE)
-        arrived(C_OUT, p)
+            message(Z_OUT + 1, p, z_out.at[1], z_in.at[1], behind(-1)).start()
+
+    for p in range(pieces(Z_OUT)):
+        rows = slice(p * size, (p + 1) * size)
+        for q in within(Z_OUT, p, C_OUT):
+            arrived(C_OUT, q)
         total = part[slot_of(0, 0, 0), rows].astype(f32) + c_in[0, rows].astype(f32)
         for d in (1, 3, 2):
-            arrived(X_OUT + (d - 1) * 2, p)
+            for q in within(Z_OUT, p, X_OUT):
+                arrived(X_OUT + (d - 1) * 2, q)
             total = total + x_in[(d - 1) * 2, rows].astype(f32)
-        z_out[0, rows] = total.astype(bf16)
+        total_acc[rows] = total
+
+        @pl.when(exists(1) & exists(-1))
+        def _():
+            arrived(Z_OUT + 1, p)
+            total_acc[rows] += z_in[1, rows].astype(f32)
+
+        z_out[0, rows] = total_acc[rows].astype(bf16)
 
         @pl.when(exists(-1))
         def _():
             message(Z_OUT, p, z_out.at[0], z_in.at[0], behind(-1)).start()
 
-    for steps in (2, 1):
-        @pl.when(exists(steps))
-        def _():
-            for p in range(PIECES):
-                rows = slice(p * PIECE, (p + 1) * PIECE)
-                arrived(Z_OUT + steps - 1, p)
-                diag[rows] += z_in[steps - 1, rows].astype(f32)
+    def left(number):
+        for p in range(pieces(number)):
+            message(number, p, own, z_in.at[0], partner).wait_send()
+
+    for number in range(X_IN, Z_OUT):
+        left(number)
+    for steps in (1, 2):
+        @pl.when(exists(1) & exists(1 - steps))
+        def _():
+            left(Z_IN + steps - 1)
+
+    @pl.when(exists(1))
+    def _():
+        for p in range(pieces(Z_OUT)):
+            rows = slice(p * size, (p + 1) * size)
+            arrived(Z_OUT, p)
+            diag[rows] += z_in[0, rows].astype(f32)
 
     outs[:TOKENS, :] = (diag[:, :WIDTH] * SCALE).astype(bf16)
     outs[TOKENS : 2 * TOKENS, :] = diag[:, WIDTH:].astype(bf16)
@@ -398,23 +439,13 @@
     ]
     for copy in last:
         copy.start()
+    for steps in (1, 2):
+        @pl.when(exists(-steps))
+        def _():
+            left(Z_OUT + steps - 1)
+
     for copy in [store] + last:
         copy.wait()
-
-    def left(number):
-        for p in range(PIECES):
-            message(number, p, own, z_in.at[0], partner).wait_send()
-
-    for number in range(X_IN, Z_OUT):
-        left(number)
-    for steps in (1, 2):
-        @pl.when(exists(1) & exists(1 - steps))
-        def _():
-            left(Z_IN + steps - 1)
-
-        @pl.when(exists(-steps))
-        def _():
-            left(Z_OUT + steps - 1)
 
 
 def hand_over(dq_in, dk_in, dv_in, dq_out, dk_out, dv_out):
@@ -452,6 +483,7 @@
             pltpu.VMEM((WIDTH, KEYS), f32),
             pltpu.VMEM((WIDTH, 2 * WIDTH), f32),
             pltpu.VMEM(chunk, f32),
+            pltpu.VMEM(chunk, f32),
             pltpu.VMEM((16,) + chunk, bf16),
             pltpu.VMEM((8,) + chunk, bf16),
             pltpu.VMEM((6,) + chunk, bf16),
@@ -459,8 +491,8 @@
             pltpu.VMEM((2,) + chunk, bf16),
             pltpu.VMEM((2,) + chunk, bf16),
             pltpu.VMEM((ROWS, WIDTH), bf16),
-            pltpu.SemaphoreType.DMA((MESSAGES * PIECES,)),
-            pltpu.SemaphoreType.DMA((MESSAGES * PIECES,)),
+            pltpu.SemaphoreType.DMA((MESSAGES * MOST,)),
+            pltpu.SemaphoreType.DMA((MESSAGES * MOST,)),
             pltpu.SemaphoreType.DMA((6,)),
             pltpu.SemaphoreType.DMA((3,)),
         ],

time: 46.9 us -> 45.7 us (0.974)
  the two profiles are of different devices: /device:TPU:24 before, /device:TPU:26 now
where the time goes in v4:
time: 45.7 us; the launch traced here: 45.6 us
  Pallas kernels  45 us (98%)
  between operations  0.64 us (1%)
    pallas_call x1, Pallas kernels, per_device(): pl.pallas_call(kernel, out_shape=shapes, in_specs=[pl.BlockSpec(memory_sp...  43.1 us
    pallas_call x1, Pallas kernels, per_device(): pl.pallas_call(hand_over, out_shape=shapes, in_specs=[pl.BlockSpec(memory...  1.81 us

profile of v4, /device:TPU:26, one launch (start us, length us, event | category | flops | bytes accessed | tf_op | source)
XLA Modules:
  0.0 45.6 jit_solution(8888093715879489500)
XLA Ops:
  0.6 43.1 %shard_map.94 = (bf16[1536,128]{1,0:T(8,128)(2,1)}, bf16[192,128]{1,0:T(8,128)(2,1)}, bf16[192,128]{1,0:T(8,128)(2,1)}) custom-call(s32[32]{0:T(128)} %len_ref.1, bf16[1536,128]{1,0:T(8,128)(2,1)} %bitcast.4, bf16[192,128]{1,0:T(8,128)(2,1)} %k_ref.1, bf16[192,128]{1,0:T(8,128)(2,1)} %v_ref.1, bf16[1536,128]{1,0:T(8,128)(2,1)} %bitcast.5, ...), custom_call_target="tpu_custom_call" | custom-call | tf_op jit(solution)/shard_map/pallas_call | solution.py:465
  43.8 1.8 %shard_map.95 = (bf16[1536,128]{1,0:T(8,128)(2,1)}, bf16[192,128]{1,0:T(8,128)(2,1)}, bf16[192,128]{1,0:T(8,128)(2,1)}) custom-call(bf16[1536,128]{1,0:T(8,128)(2,1)} %get-tuple-element.9.dq_in, bf16[192,128]{1,0:T(8,128)(2,1)} %get-tuple-element.10.dk_in, bf16[192,128]{1,0:T(8,128)(2,1)} %get-tuple-element.11.dv_in), custom_call_target="tpu_custom_call" | custom-call | tf_op jit(solution)/shard_map/pallas_call | solution.py:511

commit v5 on v4

--- a/solution.py
+++ b/solution.py
@@ -229,7 +229,6 @@
 
         for d in (1, 3, 2):
             along_x(d, 0, p, before)
-    for p in range(pieces(C_IN)):
         across(0, 0, p, before)
 
     own_keys = jnp.concatenate([own[:, :WIDTH], key_features(here)], axis=1)
@@ -316,8 +315,6 @@
     group = [(0, 0)]
     assemble(group)
     compute(group, 0)
-    compute(group, 1)
-    give(group)
     before_that = slots.at[slot_of(0, 1, 0)]
     for p in range(pieces(X_IN)):
         @pl.when(exists(-2))
@@ -335,6 +332,8 @@
         for p in range(pieces(C_IN)):
             across(0, 1, p, before_that)
 
+    compute(group, 1)
+    give(group)
     pass_on(1, 0)
     pass_on(3, 0)
     group = [(1, 0), (3, 0)]

time: 45.7 us -> 45.3 us (level)
  the two profiles are of different devices: /device:TPU:26 before, /device:TPU:24 now
where the time goes in v5:
time: 45.3 us; the launch traced here: 44.4 us
  Pallas kernels  43.8 us (97%)
  between operations  0.64 us (1%)
    pallas_call x1, Pallas kernels, per_device(): pl.pallas_call(kernel, out_shape=shapes, in_specs=[pl.BlockSpec(memory_sp...  42 us
    pallas_call x1, Pallas kernels, per_device(): pl.pallas_call(hand_over, out_shape=shapes, in_specs=[pl.BlockSpec(memory...  1.81 us

profile of v5, /device:TPU:24, one launch (start us, length us, event | category | flops | bytes accessed | tf_op | source)
XLA Modules:
  0.0 44.4 jit_solution(5298188454420560504)
XLA Ops:
  0.6 42.0 %shard_map.94 = (bf16[1536,128]{1,0:T(8,128)(2,1)}, bf16[192,128]{1,0:T(8,128)(2,1)}, bf16[192,128]{1,0:T(8,128)(2,1)}) custom-call(s32[32]{0:T(128)} %len_ref.1, bf16[1536,128]{1,0:T(8,128)(2,1)} %bitcast.4, bf16[192,128]{1,0:T(8,128)(2,1)} %k_ref.1, bf16[192,128]{1,0:T(8,128)(2,1)} %v_ref.1, bf16[1536,128]{1,0:T(8,128)(2,1)} %bitcast.5, ...), custom_call_target="tpu_custom_call" | custom-call | tf_op jit(solution)/shard_map/pallas_call | solution.py:464
  42.6 1.8 %shard_map.95 = (bf16[1536,128]{1,0:T(8,128)(2,1)}, bf16[192,128]{1,0:T(8,128)(2,1)}, bf16[192,128]{1,0:T(8,128)(2,1)}) custom-call(bf16[1536,128]{1,0:T(8,128)(2,1)} %get-tuple-element.9.dq_in, bf16[192,128]{1,0:T(8,128)(2,1)} %get-tuple-element.10.dk_in, bf16[192,128]{1,0:T(8,128)(2,1)} %get-tuple-element.11.dv_in), custom_call_target="tpu_custom_call" | custom-call | tf_op jit(solution)/shard_map/pallas_call | solution.py:510
